TPU v7x, 768 devices: a whole 4x8x12 slice. The times are simulated.
768 devices in a mesh: dom: 12 (over z), work: 64 (over y, x, core).
Axes of the slice: x: 4, y: 8, z: 12, core: 2. Of those that a mesh axis runs over, the one named last changes fastest.
Arguments:
- embeddings: float32 [12288, 400], P(('dom', 'work'))
- adagrad: float32 [12288], P(('dom', 'work')), may hold values from 0.05 to 1
- plan: int32 [12], replicated, may hold values from 0 to 11, each once
- src_ids: int32 [12, 64, 512], P('dom', 'work'), may hold values from 0 to 1023
- dst_ids: int32 [12, 64, 512], P('dom', 'work'), may hold values from 0 to 1023
- neg_ids: int32 [12, 64, 512], P('dom', 'work'), may hold values from 0 to 511
- counts: int32 [12, 64], P('dom', 'work'), may hold values from 64 to 512, as said below
Outputs:
- new_embeddings: float32 [12288, 400], P(('dom', 'work'))
- new_adagrad: float32 [12288], P(('dom', 'work'))
Inputs may be any that keep to these rules, and one draw needn't show every extreme that they name: plan is a permutation of the partitions. `counts`: some worker's block is full in every draw.
All inputs are finite; a program needn't handle non-finite values.
Results may differ from a plain program's by a relative error of at most 0.0003.
Values sent between devices are 32-bit elements; how exact they have to be, the bound alone decides.
No kernel may reach another device: no remote copies, remote signals or barrier semaphores. Data moves between devices by JAX's collectives and lax.ppermute only.
A program may use at most 32 MiB of HBM per device.

v0:
```python
import jax
import jax.numpy as jnp
from jax import lax
from jax.sharding import PartitionSpec as P

learn_rate = 0.1
epsilon = 1e-08


def take_rows(piece, wanted):
    inside = (wanted >= 0) & (wanted < piece.shape[0])
    found = jnp.take(piece, jnp.clip(wanted, 0, piece.shape[0] - 1), axis=0)
    return jnp.where(inside[:, None], found, 0.0)


def spread_rows(values, wanted, count):
    inside = (wanted >= 0) & (wanted < count)
    target = jnp.where(inside, wanted, count)
    return jnp.zeros((count, values.shape[1]), jnp.float32).at[target].add(values, mode="drop")


def softmax_weights(positive, scores, live_count):
    logits = jnp.concatenate([positive[:, None], scores], axis=1)
    row_max = jnp.max(logits, axis=1, keepdims=True)
    shifted = jnp.exp(logits - row_max)
    probabilities = shifted / jnp.sum(shifted, axis=1, keepdims=True)
    live_mask = (jnp.arange(positive.shape[0], dtype=jnp.int32) < live_count).astype(jnp.float32)
    pos_weight = (probabilities[:, 0] - 1.0) * live_mask
    neg_weight = probabilities[:, 1:] * live_mask[:, None]
    return (pos_weight, neg_weight)


def matmul(left, right):
    return jnp.dot(left, right, precision=lax.Precision.HIGHEST, preferred_element_type=jnp.float32)


def body(embeddings, adagrad, plan, src_ids, dst_ids, neg_ids, counts):
    shard_rows = embeddings.shape[0]
    dom_index = lax.axis_index("dom")
    right_part = plan[dom_index]
    sender = jnp.sum(jnp.where(plan == dom_index, jnp.arange(plan.shape[0], dtype=jnp.int32), 0))
    src_local = src_ids[0, 0]
    dst_local = dst_ids[0, 0]
    neg_slots = neg_ids[0, 0]
    live_count = counts[0, 0]
    shards = lax.all_gather(embeddings, "dom", axis=0, tiled=True)
    partner = lax.dynamic_slice_in_dim(shards, right_part * shard_rows, shard_rows, 0)
    src_rows = take_rows(lax.all_gather(embeddings, "work", axis=0, tiled=True), src_local)
    dst_rows = take_rows(lax.all_gather(partner, "work", axis=0, tiled=True), dst_local)
    positive = jnp.sum(src_rows * dst_rows, axis=1)
    neg_rows = jnp.take(dst_rows, neg_slots, axis=0)
    scores = matmul(src_rows, neg_rows.T)
    pos_weight, neg_weight = softmax_weights(positive, scores, live_count)
    src_grad = pos_weight[:, None] * dst_rows + matmul(neg_weight, neg_rows)
    neg_grad = matmul(neg_weight.T, src_rows)
    dst_grad = pos_weight[:, None] * src_rows + jnp.zeros_like(dst_rows).at[neg_slots].add(neg_grad)
    left_grads = lax.psum_scatter(
        spread_rows(src_grad, src_local, lax.axis_size("work") * shard_rows),
        "work",
        scatter_dimension=0,
        tiled=True,
    )
    right_grads = lax.psum_scatter(
        spread_rows(dst_grad, dst_local, lax.axis_size("work") * shard_rows),
        "work",
        scatter_dimension=0,
        tiled=True,
    )
    gathered = lax.all_gather(right_grads, "dom", axis=0, tiled=True)
    back_grads = lax.dynamic_slice_in_dim(gathered, sender * shard_rows, shard_rows, 0)
    grads = left_grads + back_grads
    new_adagrad = adagrad + jnp.mean(grads * grads, axis=1)
    new_embeddings = embeddings - learn_rate * grads / (jnp.sqrt(new_adagrad)[:, None] + epsilon)
    return (new_embeddings, new_adagrad)


def solution(mesh):
    in_specs = (
        P(("dom", "work"), None),
        P(("dom", "work")),
        P(),
        P("dom", "work", None),
        P("dom", "work", None),
        P("dom", "work", None),
        P("dom", "work"),
    )
    out_specs = (P(("dom", "work"), None), P(("dom", "work")))
    return jax.shard_map(body, mesh=mesh, in_specs=in_specs, out_specs=out_specs, check_vma=False)
```

profile of v0, /device:TPU:16, one launch (start us, length us, event | category | flops | bytes accessed | tf_op | source)
XLA Modules:
  0.0 546.4 jit_solution(361309923505402693)
XLA Ops:
  8.0 1.2 dynamic_slice.9
  9.9 34.6 %all_gather.13 = f32[192,400]{1,0:T(8,128)S(1)} all-gather(f32[16,400]{1,0:T(8,128)} %param.9), channel_id=1, replica_groups=mesh['dom'=12,'work'=64] {'dom'}, dimensions={0}, use_global_device_ids=true | all-gather | bytes 332800 | tf_op jit(solution)/shard_map/all_gather | solution.py:46
  47.9 0.7 and_reduce_fusion
  48.6 0.7 compare_and_fusion.2
  50.0 56.3 %all-gather.3.cloned.1.call-done = f32[1024,400]{1,0:T(8,128)} async-done(((f32[16,400]{1,0:T(8,128)}), f32[1024,400]{1,0:T(8,128)}) %all-gather.3.cloned.1.call-update) | async-done | bytes 1638416 | tf_op jit(solution)/shard_map/all_gather | solution.py:48
  106.3 3.6 gather_fusion.1
  110.3 86.7 %all-gather.5.cloned.1.call-done = f32[1024,400]{1,0:T(8,128)} async-done(((f32[16,400]{1,0:T(8,128)}), f32[1024,400]{1,0:T(8,128)}) %all-gather.5.cloned.1.call-update) | async-done | bytes 1638416 | tf_op jit(solution)/shard_map/all_gather | solution.py:49
  196.9 3.6 gather_fusion.2
  201.1 0.9 copy-done.2
  202.3 1.6 gather_fusion
  203.9 1.9 fusion.33
  206.4 1.9 fusion.8
  208.3 1.0 fusion.11
  209.4 1.5 copy.16
  210.8 4.2 scatter_fusion
  215.0 5.0 scatter_custom_fusion.2
  221.5 3.2 convolution_add_fusion
  224.7 1.5 copy.15
  226.2 5.0 scatter_custom_fusion
  233.1 142.3 %reduce-scatter.5.cloned.1.call-done = f32[16,400]{1,0:T(8,128)} async-done(((f32[1024,400]{1,0:T(8,128)}), f32[16,400]{1,0:T(8,128)}) %reduce-scatter.5.cloned.1.call-update) | async-done | bytes 25616 | tf_op jit(solution)/shard_map/reduce_scatter | solution.py:63
  375.3 26.5 %all_gather.15 = f32[192,400]{1,0:T(8,128)S(1)} all-gather(f32[16,400]{1,0:T(8,128)} %reduce-scatter.5.cloned.1.call-done), channel_id=1, replica_groups=mesh['dom'=12,'work'=64] {'dom'}, dimensions={0}, use_global_device_ids=true | all-gather | bytes 332800 | tf_op jit(solution)/shard_map/all_gather | solution.py:69
  401.9 135.1 %reduce-scatter.3.cloned.1.call-done = f32[16,400]{1,0:T(8,128)} async-done(((f32[1024,400]{1,0:T(8,128)}), f32[16,400]{1,0:T(8,128)}) %reduce-scatter.3.cloned.1.call-update) | async-done | bytes 25616 | tf_op jit(solution)/shard_map/reduce_scatter | solution.py:57
  537.0 0.9 multiply_reduce_fusion.1
  538.4 1.5 divide_subtract_fusion
  (46 shorter events, 9.1 us)
Async XLA Ops:
  7.2 99.2 %all-gather.3.cloned.1.call-start = ((), (), s32[]{:S(2)}) async-start(), calls=%async_computation.2 | async-start | bytes 2129920 | tf_op jit(solution)/shard_map/all_gather | solution.py:48
  7.9 189.0 %all-gather.5.cloned.1.call-start = ((), (), s32[]{:S(2)}) async-start(), calls=%async_computation.3 | async-start | bytes 2129920 | tf_op jit(solution)/shard_map/all_gather | solution.py:49
  45.1 330.2 %reduce-scatter.5.cloned.1.call-start = ((), (), s32[]{:S(2)}) async-start(), calls=%async_computation.5 | async-start | bytes 2129920 | tf_op jit(solution)/shard_map/reduce_scatter | solution.py:63
  201.1 0.9 copy-start.2
  206.4 2.0 copy-start
  220.0 0.7 copy-start.5
  220.0 1.2 copy-start.1
  220.0 1.5 copy-start.3
  220.1 316.9 %reduce-scatter.3.cloned.1.call-start = ((), (), s32[]{:S(2)}) async-start(), calls=%async_computation.4 | async-start | bytes 2129920 | tf_op jit(solution)/shard_map/reduce_scatter | solution.py:57
  231.1 0.7 copy-start.7
  231.1 306.8 %copy-start.6 = (f32[16]{0:T(128)S(1)}, f32[16]{0:T(128)}, u32[]{:S(2)}) copy-start(f32[16]{0:T(128)} %param.10) | copy-start | bytes 196
  231.1 307.3 %copy-start.4 = (f32[16,400]{1,0:T(8,128)S(1)}, f32[16,400]{1,0:T(8,128)}, u32[]{:S(2)}) copy-start(f32[16,400]{1,0:T(8,128)} %param.9) | copy-start | bytes 76804
Sparse Core Ops, SparseCore 0:
  11.9 94.3 all-gather.2
  110.8 86.0 all-gather.4
  220.2 155.0 reduce-scatter.4
  381.2 155.7 reduce-scatter.2
where the time goes:
time: 547 us; the launch traced here: 546 us
  waiting for transfers between devices  421 us (77%)
  blocking collectives  61.2 us (11%)
  other arithmetic  23.5 us (4%)
  local copies, waits for them, and re-layouts  17.5 us (3%)
  between operations  15.9 us (3%)
  matrix products  7.03 us (1%)
    reduce_scatter x1, waiting for transfers between devices, body(): lax.psum_scatter(spread_rows(dst_grad, dst_local, lax.axis_size('work') *...  142 us
    reduce_scatter x1, waiting for transfers between devices, body(): lax.psum_scatter(spread_rows(src_grad, src_local, lax.axis_size('work') *...  135 us
    all_gather x1, waiting for transfers between devices, body(): lax.all_gather(partner, 'work', axis=0, tiled=True)  86.7 us
    all_gather x1, waiting for transfers between devices, body(): lax.all_gather(embeddings, 'work', axis=0, tiled=True)  56.3 us
    all_gather x1, blocking collectives, body(): shards = lax.all_gather(embeddings, 'dom', axis=0, tiled=True)  34.6 us
    all_gather x1, blocking collectives, body(): gathered = lax.all_gather(right_grads, 'dom', axis=0, tiled=True)  26.5 us
  transfers between devices with their start and end apart: 4, of which 4 were waited for; matrix products, arithmetic and copies ran while one was open for 4% of the time, Pallas kernels for 0%

commit v1 on v0

v1 whole, which is shorter than its diff:
```python
import jax
import jax.numpy as jnp
from jax import lax
from jax.experimental import pallas as pl
from jax.experimental.pallas import tpu as pltpu
from jax.sharding import Mesh, PartitionSpec as P

learn_rate = 0.1
epsilon = 1e-08

DOM, NY, NX, NC = 12, 8, 4, 2
D = 400
WIDE = 512
SHARD = 16
META = 8
PAY = SHARD + META
SLOTS = 512
LANES = 128
HALF = NX * NY
HI = lax.Precision.HIGHEST
NT = (((1,), (1,)), ((), ()))
TN = (((0,), (0,)), ((), ()))


def whole(space=pltpu.VMEM):
    return pl.BlockSpec(memory_space=space)


def pack_kernel(count_ref, emb_ref, src_ref, dst_ref, neg_ref, out_ref):
    out_ref[...] = jnp.zeros_like(out_ref)
    out_ref[0:SHARD, 0:D] = emb_ref[...]
    slot = lax.broadcasted_iota(jnp.int32, (1, SLOTS), 1)
    src = jnp.where(slot < count_ref[0], src_ref[...], -1)
    dst, neg = dst_ref[...], neg_ref[...]
    place = (((dst >> 4) & 1) << 9) | (((dst >> 5) & 3) << 7) | ((dst >> 7) << 4) | (dst & 15)
    high = lax.broadcasted_iota(jnp.int32, (8, SLOTS), 0)
    low = lax.broadcasted_iota(jnp.int32, (LANES, SLOTS), 0)
    uses = lax.dot_general(
        jnp.where((neg >> 7) == high, 1.0, 0.0),
        jnp.where((neg & 127) == low, 1.0, 0.0),
        NT,
        precision=HI,
        preferred_element_type=jnp.float32,
    )
    uses = jnp.concatenate([uses[r : r + 1] for r in range(4)], axis=1)
    table = lax.dot_general(
        jnp.where((place >> 7) == high, uses, 0.0),
        jnp.where((place & 127) == low, 1.0, 0.0),
        NT,
        precision=HI,
        preferred_element_type=jnp.float32,
    )
    out_ref[SHARD:PAY, 0:LANES] = table
    src, place = src.astype(jnp.float32), place.astype(jnp.float32)
    for r in range(4):
        cut = slice(r * LANES, (r + 1) * LANES)
        out_ref[SHARD + r : SHARD + r + 1, LANES : 2 * LANES] = src[:, cut]
        out_ref[SHARD + 4 + r : SHARD + 5 + r, LANES : 2 * LANES] = place[:, cut]


def pair_kernel(where_ref, left_ref, own_ref, oth_ref, dleft_ref, down_ref, doth_ref, m_ref):
    worker, core = where_ref[0], where_ref[1]
    left = left_ref[...]

    def rows(ref):
        return ref[:, 0:SHARD, :].reshape(HALF * SHARD, WIDE)

    def dot(a, b, dims=(((1,), (0,)), ((), ()))):
        return lax.dot_general(a, b, dims, precision=HI, preferred_element_type=jnp.float32)

    s_own, s_oth = dot(left, rows(own_ref), NT), dot(left, rows(oth_ref), NT)
    first = core == 0
    s_low = jnp.where(first, s_own, s_oth)
    s_high = jnp.where(first, s_oth, s_own)
    logits = jnp.stack(
        [half[:, r * LANES : (r + 1) * LANES] for half in (s_low, s_high) for r in range(4)]
    )
    m_ref[...] = jnp.zeros_like(m_ref)
    step_rows = lax.broadcasted_iota(jnp.int32, (LANES, SLOTS), 0)

    def over_blocks(ref):
        def block(b, carry):
            meta = ref[b, SHARD:PAY, 0 : 2 * LANES]
            table = meta[:, 0:LANES]
            lists = meta[:, LANES : 2 * LANES].astype(jnp.int32)
            src = jnp.concatenate([lists[r : r + 1] for r in range(4)], axis=1) - worker * SHARD
            dst = jnp.concatenate([lists[r : r + 1] for r in range(4, 8)], axis=1)
            mine = (src >= 0) & (src < SHARD)
            code = jnp.where(mine, ((dst >> 7) << 4) + src, -1)
            at_pair = jnp.where(code == step_rows, 1.0, 0.0).astype(jnp.bfloat16)
            at_low = jnp.where((dst & 127) == step_rows, 1.0, 0.0).astype(jnp.bfloat16)
            edges = lax.dot_general(at_pair, at_low, NT, preferred_element_type=jnp.float32)
            edges = edges.reshape(8, SHARD, LANES)
            counts = jnp.broadcast_to(table[:, None, :], (8, SHARD, LANES))
            masked = jnp.where(counts > 0.0, logits, -jnp.inf)
            top = jnp.max(jnp.max(masked, axis=0), axis=1, keepdims=True)[None]
            weights = counts * jnp.exp(masked - top)
            total = jnp.sum(jnp.sum(weights, axis=0), axis=1, keepdims=True)[None]
            gap = logits - top
            small = jnp.exp(-jnp.abs(gap))
            above = gap >= 0.0
            pos = jnp.where(above, 1.0, small)
            neg = jnp.where(above, small, 1.0)
            share = edges * neg / (pos + total * neg)
            sums = jnp.sum(jnp.sum(share, axis=0), axis=1, keepdims=True)[None]
            m_ref[...] += sums * weights - total * share
            return carry

        lax.fori_loop(0, HALF, block, 0, unroll=2)

    over_blocks(own_ref)
    over_blocks(oth_ref)
    m = m_ref[...]
    m_low = jnp.concatenate([m[r] for r in range(4)], axis=1)
    m_high = jnp.concatenate([m[r] for r in range(4, 8)], axis=1)
    m_own = jnp.where(first, m_low, m_high)
    m_oth = jnp.where(first, m_high, m_low)
    dleft_ref[...] = dot(m_own, rows(own_ref)) + dot(m_oth, rows(oth_ref))
    down_ref[...] = dot(m_own, left, TN)
    doth_ref[...] = dot(m_oth, left, TN)


def to_all(piece, axis, size):
    return lax.all_to_all(jnp.tile(piece, (size, 1)), axis, 0, 0, tiled=True)


def swap_core(piece):
    return lax.ppermute(piece, "c", [(0, 1), (1, 0)])


def summed(piece, axis, size):
    got = lax.all_to_all(piece, axis, 0, 0, tiled=True)
    return jnp.sum(got.reshape(size, -1, got.shape[1]), axis=0)


def body(embeddings, adagrad, plan, src_ids, dst_ids, neg_ids, counts):
    part = lax.axis_index("dom")
    core = lax.axis_index("c")
    worker = (lax.axis_index("y") * NX + lax.axis_index("x")) * NC + core
    sender = jnp.sum(jnp.where(plan == part, jnp.arange(DOM, dtype=jnp.int32), 0))
    f32 = jnp.float32

    own = pl.pallas_call(
        pack_kernel,
        out_shape=jax.ShapeDtypeStruct((PAY, WIDE), f32),
        in_specs=[whole(pltpu.SMEM)] + [whole()] * 4,
        out_specs=whole(),
        name="pack",
    )(counts[0], embeddings, src_ids[0], dst_ids[0], neg_ids[0])

    came = to_all(own, "dom", DOM)
    came = lax.dynamic_slice_in_dim(came, sender * PAY, PAY, 0)
    payload = jnp.concatenate([own[:SHARD], came[SHARD:]], axis=0)
    near = to_all(to_all(payload, "y", NY), "x", NX)
    far = swap_core(near)

    dleft, down, doth = pl.pallas_call(
        pair_kernel,
        out_shape=(
            jax.ShapeDtypeStruct((SHARD, WIDE), f32),
            jax.ShapeDtypeStruct((HALF * SHARD, WIDE), f32),
            jax.ShapeDtypeStruct((HALF * SHARD, WIDE), f32),
        ),
        in_specs=[whole(pltpu.SMEM)] + [whole()] * 3,
        out_specs=(whole(),) * 3,
        scratch_shapes=[pltpu.VMEM((8, SHARD, LANES), f32)],
        compiler_params=pltpu.CompilerParams(vmem_limit_bytes=40 * 1024 * 1024),
        name="pair",
    )(
        jnp.stack([worker, core]).astype(jnp.int32),
        came[:SHARD],
        near.reshape(HALF, PAY, WIDE),
        far.reshape(HALF, PAY, WIDE),
    )

    right = summed(summed(down + swap_core(doth), "x", NX), "y", NY)
    back = to_all(dleft, "dom", DOM)
    back = lax.dynamic_slice_in_dim(back, plan[part] * SHARD, SHARD, 0)
    grads = (right + back)[:, :D]
    new_adagrad = adagrad + jnp.mean(grads * grads, axis=1)
    new_embeddings = embeddings - learn_rate * grads / (jnp.sqrt(new_adagrad)[:, None] + epsilon)
    return (new_embeddings, new_adagrad)


def solution(mesh):
    axes = ("dom", "y", "x", "c")
    grid = Mesh(mesh.devices.reshape(DOM, NY, NX, NC), axes)
    edge = P("dom", ("y", "x", "c"), None)
    in_specs = (P(axes, None), P(axes), P(), edge, edge, edge, P("dom", ("y", "x", "c")))
    out_specs = (P(axes, None), P(axes))
    return jax.shard_map(body, mesh=grid, in_specs=in_specs, out_specs=out_specs, check_vma=False)
```

time: 547 us -> 174 us (0.32)
  the two profiles are of different devices: /device:TPU:16 before, /device:TPU:64 now
where the time goes in v1:
time: 174 us; the launch traced here: 173 us
  blocking collectives  76.9 us (44%)
  waiting for transfers between devices  46.2 us (27%)
  starting transfers between devices  22.2 us (13%)
  Pallas kernels  18.8 us (11%)
  local copies, waits for them, and re-layouts  4.14 us (2%)
  between operations  2.7 us (2%)
  other arithmetic  2.35 us (1%)
    all_to_all x2, blocking collectives, to_all(): return lax.all_to_all(jnp.tile(piece, (size, 1)), axis, 0, 0, tiled=True)  44.8 us
    all_to_all x2, waiting for transfers between devices, to_all(): return lax.all_to_all(jnp.tile(piece, (size, 1)), axis, 0, 0, tiled=True)  41.2 us
    all_to_all x2, blocking collectives, summed(): got = lax.all_to_all(piece, axis, 0, 0, tiled=True)  32.1 us
    all_to_all x2, starting transfers between devices, to_all(): return lax.all_to_all(jnp.tile(piece, (size, 1)), axis, 0, 0, tiled=True)  18.3 us
    pallas_call x1, Pallas kernels, body(): pl.pallas_call(pair_kernel, out_shape=(jax.ShapeDtypeStruct((SHARD, WIDE)...  16.4 us
    ppermute x2, waiting for transfers between devices, swap_core(): return lax.ppermute(piece, 'c', [(0, 1), (1, 0)])  5.03 us
    ppermute x2, starting transfers between devices, swap_core(): return lax.ppermute(piece, 'c', [(0, 1), (1, 0)])  3.96 us
  transfers between devices with their start and end apart: 4, of which 4 were waited for; matrix products, arithmetic and copies ran while one was open for 1% of the time, Pallas kernels for 0%

profile of v1, /device:TPU:64, one launch (start us, length us, event | category | flops | bytes accessed | tf_op | source)
XLA Modules:
  0.0 173.3 jit_solution(7058812193979809748)
XLA Ops:
  1.3 2.4 %pack.1 = f32[24,512]{1,0:T(8,128)} custom-call(s32[1]{0:T(128)} %bitcast.15.count_ref, f32[16,400]{1,0:T(8,128)} %emb_ref.1, s32[1,512]{1,0:T(1,128)} %bitcast.26, s32[1,512]{1,0:T(1,128)} %bitcast.27, s32[1,512]{1,0:T(1,128)} %bitcast.28), custom_call_target="tpu_custom_call" | custom-call | tf_op jit(solution)/shard_map/pack/pallas_call | solution.py:143
  3.7 1.7 %tile.10 = f32[12,24,512]{2,1,0:T(8,128)} broadcast(f32[24,512]{1,0:T(8,128)} %pack.1), dimensions={1,2} | broadcast | bytes 638976 | tf_op jit(solution)/shard_map/tile | solution.py:124
  5.5 14.8 %all-to-all-start = ((f32[12,24,512]{2,1,0:T(8,128)}), f32[12,24,512]{2,1,0:T(8,128)S(1)}, u32[]{:S(2)}, u32[]{:S(2)}) async-start(f32[12,24,512]{2,1,0:T(8,128)} %tile.10), calls=%async_computation | async-start | bytes 1179648 | tf_op jit(solution)/shard_map/all_to_all | solution.py:124
  20.2 0.6 fusion
  21.5 24.9 %all-to-all-done = f32[12,24,512]{2,1,0:T(8,128)S(1)} async-done(((f32[12,24,512]{2,1,0:T(8,128)}), f32[12,24,512]{2,1,0:T(8,128)S(1)}, u32[]{:S(2)}, u32[]{:S(2)}) %all-to-all-start) | async-done | bytes 589856 | tf_op jit(solution)/shard_map/all_to_all | solution.py:124
  46.5 21.5 %all_to_all.51 = f32[8,24,512]{2,1,0:T(8,128)S(1)} all-to-all(f32[8,24,512]{2,1,0:T(8,128)S(1)} %tile.11), channel_id=1, replica_groups=mesh['dom'=12,'y'=8,'x'=4,'c'=2] {'y'}, dimensions={0} | all-to-all | bytes 786432 | tf_op jit(solution)/shard_map/all_to_all | solution.py:124
  67.9 0.2 tile.13
  68.1 23.3 %all_to_all.52 = f32[4,192,512]{2,1,0:T(8,128)S(1)} all-to-all(f32[4,192,512]{2,1,0:T(8,128)S(1)} %tile.13), channel_id=1, replica_groups=mesh['dom'=12,'y'=8,'x'=4,'c'=2] {'x'}, dimensions={0} | all-to-all | bytes 3145728 | tf_op jit(solution)/shard_map/all_to_all | solution.py:124
  91.4 1.9 %collective-permute-start = (f32[768,512]{1,0:T(8,128)S(1)}, f32[768,512]{1,0:T(8,128)S(1)}, u32[]{:S(2)}, u32[]{:S(2)}) collective-permute-start(f32[768,512]{1,0:T(8,128)S(1)} %bitcast.16), channel_id=1, source_target_pairs={{0,1},{1,0},{2,3},{3,2},{4,5},{5,4},{6,7},{7,6},{8,9},{9,8},{10,11... | collective-permute-start | bytes 4718600 | tf_op jit(solution)/shard_map/ppermute | solution.py:128
  93.4 0.8 constant_dynamic-slice_fusion.left_ref
  94.2 2.5 %collective-permute-done = f32[768,512]{1,0:T(8,128)S(1)} collective-permute-done((f32[768,512]{1,0:T(8,128)S(1)}, f32[768,512]{1,0:T(8,128)S(1)}, u32[]{:S(2)}, u32[]{:S(2)}) %collective-permute-start) | collective-permute-done | bytes 1572896 | tf_op jit(solution)/shard_map/ppermute | solution.py:128
  96.7 16.4 %pair.1 = (f32[16,512]{1,0:T(8,128)S(1)}, f32[512,512]{1,0:T(8,128)S(1)}, f32[512,512]{1,0:T(8,128)S(1)}) custom-call(s32[2]{0:T(128)S(1)} %pad_add_fusion.where_ref, f32[16,512]{1,0:T(8,128)S(1)} %constant_dynamic-slice_fusion.left_ref, f32[32,24,512]{2,1,0:T(8,128)S(1)} %bitcast.17, f32[32,24,512]{2,1,0:T(8,128)S(1)} %bitcast.18), custom_call_target="tpu_custom_call" | custom-call | tf_op jit(solution)/shard_map/pair/pallas_call | solution.py:157
  113.1 2.0 %collective-permute-start.1 = (f32[512,512]{1,0:T(8,128)S(1)}, f32[512,512]{1,0:T(8,128)S(1)}, u32[]{:S(2)}, u32[]{:S(2)}) collective-permute-start(f32[512,512]{1,0:T(8,128)S(1)} %get-tuple-element.6), channel_id=1, source_target_pairs={{0,1},{1,0},{2,3},{3,2},{4,5},{5,4},{6,7},{7,6},{8,9},{9,8},{10,11... | collective-permute-start | bytes 3145736 | tf_op jit(solution)/shard_map/ppermute | solution.py:128
  115.1 2.5 %collective-permute-done.1 = f32[512,512]{1,0:T(8,128)S(1)} collective-permute-done((f32[512,512]{1,0:T(8,128)S(1)}, f32[512,512]{1,0:T(8,128)S(1)}, u32[]{:S(2)}, u32[]{:S(2)}) %collective-permute-start.1) | collective-permute-done | bytes 1048608 | tf_op jit(solution)/shard_map/ppermute | solution.py:128
  117.6 0.2 add.31
  117.9 18.1 %all_to_all.53 = f32[4,128,512]{2,1,0:T(8,128)S(1)} all-to-all(f32[4,128,512]{2,1,0:T(8,128)S(1)} %bitcast.19), channel_id=1, replica_groups=mesh['dom'=12,'y'=8,'x'=4,'c'=2] {'x'}, dimensions={0} | all-to-all | bytes 2097152 | tf_op jit(solution)/shard_map/all_to_all | solution.py:132
  136.1 14.0 %all_to_all.54 = f32[8,16,512]{2,1,0:T(8,128)S(1)} all-to-all(f32[8,16,512]{2,1,0:T(8,128)S(1)} %bitcast.21), channel_id=1, replica_groups=mesh['dom'=12,'y'=8,'x'=4,'c'=2] {'y'}, dimensions={0} | all-to-all | bytes 524288 | tf_op jit(solution)/shard_map/all_to_all | solution.py:132
  150.1 0.8 tile.14
  150.9 3.5 %all-to-all-start.5 = ((f32[12,16,512]{2,1,0:T(8,128)}), f32[12,16,512]{2,1,0:T(8,128)S(1)}, u32[]{:S(2)}, u32[]{:S(2)}) async-start(f32[12,16,512]{2,1,0:T(8,128)} %tile.14), calls=%async_computation.5 | async-start | bytes 786432 | tf_op jit(solution)/shard_map/all_to_all | solution.py:124
  154.4 0.6 dynamic_slice.10
  155.7 16.3 %all-to-all-done.5 = f32[12,16,512]{2,1,0:T(8,128)S(1)} async-done(((f32[12,16,512]{2,1,0:T(8,128)}), f32[12,16,512]{2,1,0:T(8,128)S(1)}, u32[]{:S(2)}, u32[]{:S(2)}) %all-to-all-start.5) | async-done | bytes 393248 | tf_op jit(solution)/shard_map/all_to_all | solution.py:124
  172.0 0.1 multiply_reduce_fusion
  172.1 0.5 sqrt_add_fusion
  172.6 0.7 divide_subtract_fusion
  (16 shorter events, 0.2 us)
Async XLA Ops:
  0.6 19.6 %copy-start.3 = (s32[12]{0:T(128)S(1)}, s32[12]{0:T(128)}, u32[]{:S(2)}) copy-start(s32[12]{0:T(128)} %param.9) | copy-start | bytes 148
  3.7 42.7 %slice-start = ((f32[24,512]{1,0:T(8,128)}), f32[16,512]{1,0:T(8,128)S(1)}, s32[]{:S(2)}) async-start(f32[24,512]{1,0:T(8,128)} %pack.1), calls=%async_computation.6 | async-start | bytes 65536 | tf_op jit(solution)/shard_map/slice | solution.py:153
  5.5 40.9 %all-to-all-start = ((f32[12,24,512]{2,1,0:T(8,128)}), f32[12,24,512]{2,1,0:T(8,128)S(1)}, u32[]{:S(2)}, u32[]{:S(2)}) async-start(f32[12,24,512]{2,1,0:T(8,128)} %tile.10), calls=%async_computation | async-start | bytes 1179648 | tf_op jit(solution)/shard_map/all_to_all | solution.py:124
  46.4 21.5 %copy-start = (f32[12,24,512]{2,1,0:T(8,128)}, f32[12,24,512]{2,1,0:T(8,128)S(1)}, u32[]{:S(2)}) copy-start(f32[12,24,512]{2,1,0:T(8,128)S(1)} %all-to-all-done) | copy-start | bytes 1769476
  91.4 5.3 %collective-permute-start = (f32[768,512]{1,0:T(8,128)S(1)}, f32[768,512]{1,0:T(8,128)S(1)}, u32[]{:S(2)}, u32[]{:S(2)}) collective-permute-start(f32[768,512]{1,0:T(8,128)S(1)} %bitcast.16), channel_id=1, source_target_pairs={{0,1},{1,0},{2,3},{3,2},{4,5},{5,4},{6,7},{7,6},{8,9},{9,8},{10,11... | collective-permute-start | bytes 4718600 | tf_op jit(solution)/shard_map/ppermute | solution.py:128
  113.1 4.6 %collective-permute-start.1 = (f32[512,512]{1,0:T(8,128)S(1)}, f32[512,512]{1,0:T(8,128)S(1)}, u32[]{:S(2)}, u32[]{:S(2)}) collective-permute-start(f32[512,512]{1,0:T(8,128)S(1)} %get-tuple-element.6), channel_id=1, source_target_pairs={{0,1},{1,0},{2,3},{3,2},{4,5},{5,4},{6,7},{7,6},{8,9},{9,8},{10,11... | collective-permute-start | bytes 3145736 | tf_op jit(solution)/shard_map/ppermute | solution.py:128
  136.0 36.2 %copy-start.2 = (f32[16]{0:T(128)S(1)}, f32[16]{0:T(128)}, u32[]{:S(2)}) copy-start(f32[16]{0:T(128)} %param.8) | copy-start | bytes 196
  136.0 36.7 %copy-start.1 = (f32[16,400]{1,0:T(8,128)S(1)}, f32[16,400]{1,0:T(8,128)}, u32[]{:S(2)}) copy-start(f32[16,400]{1,0:T(8,128)} %emb_ref.1) | copy-start | bytes 76804
  150.9 21.1 %all-to-all-start.5 = ((f32[12,16,512]{2,1,0:T(8,128)}), f32[12,16,512]{2,1,0:T(8,128)S(1)}, u32[]{:S(2)}, u32[]{:S(2)}) async-start(f32[12,16,512]{2,1,0:T(8,128)} %tile.14), calls=%async_computation.5 | async-start | bytes 786432 | tf_op jit(solution)/shard_map/all_to_all | solution.py:124

commit v2 on v1

v2 whole, which is shorter than its diff:
```python
import jax
import jax.numpy as jnp
from jax import lax
from jax.experimental import pallas as pl
from jax.experimental.pallas import tpu as pltpu
from jax.sharding import Mesh, PartitionSpec as P

learn_rate = 0.1
epsilon = 1e-08

DOM, NY, NX, NC = 12, 8, 4, 2
D = 400
WIDE = 512
SHARD = 16
SLOTS = 512
LANES = 128
HALF = NX * NY
ROWS = HALF * SHARD
BODY = 384
HEAD = D - BODY
HI = lax.Precision.HIGHEST
NN = (((1,), (0,)), ((), ()))
NT = (((1,), (1,)), ((), ()))
TN = (((0,), (0,)), ((), ()))
LEFT = 64
BACK = 56
BIG = 24 * 1024 * 1024


SPACES = {"s": pltpu.SMEM, "v": pltpu.VMEM}
WORKER, CORE, AT_X, SENDER, TARGET = range(5)


def whole(space=pltpu.VMEM):
    return pl.BlockSpec(memory_space=space)


def call(kernel, out, spaces, scratch=(), name=None):
    many = isinstance(out, tuple)
    return pl.pallas_call(
        kernel,
        out_shape=out,
        in_specs=[whole(SPACES[space]) for space in spaces],
        out_specs=(whole(),) * len(out) if many else whole(),
        scratch_shapes=list(scratch),
        compiler_params=pltpu.CompilerParams(vmem_limit_bytes=BIG),
        name=name,
    )


def vmem(*shape):
    return pltpu.VMEM(shape, jnp.float32)


def f32(*shape):
    return jax.ShapeDtypeStruct(shape, jnp.float32)


def hi_dot(a, b, dims=NN):
    return lax.dot_general(a, b, dims, precision=HI, preferred_element_type=jnp.float32)


def pack_kernel(count_ref, emb_ref, ids_ref, left_ref, mine_ref, out_ref):
    for ref in (left_ref, mine_ref):
        ref[...] = jnp.zeros_like(ref)
        ref[0:SHARD, 0:D] = emb_ref[...]
    slot = lax.broadcasted_iota(jnp.int32, (1, SLOTS), 1)
    src = jnp.where(slot < count_ref[0], ids_ref[0:1], -1)
    dst, neg = ids_ref[1:2], ids_ref[2:3]
    place = (((dst >> 4) & 1) << 9) | (((dst >> 5) & 3) << 7) | ((dst >> 7) << 4) | (dst & 15)
    high = lax.broadcasted_iota(jnp.int32, (8, SLOTS), 0)
    low = lax.broadcasted_iota(jnp.int32, (LANES, SLOTS), 0)
    uses = lax.dot_general(
        jnp.where((neg >> 7) == high, 1.0, 0.0),
        jnp.where((neg & 127) == low, 1.0, 0.0),
        NT,
        precision=HI,
        preferred_element_type=jnp.float32,
    )
    row = lax.broadcasted_iota(jnp.int32, (SHARD, LANES), 0)
    lane = lax.broadcasted_iota(jnp.int32, (SHARD, LANES), 1)
    out = jnp.zeros((SHARD, LANES), jnp.float32)
    for t, item in enumerate((src, place, uses)):
        if t < 2:
            item = item.astype(jnp.float32)
            item = [item[:, r * LANES : (r + 1) * LANES] for r in range(4)]
        else:
            item = [item[r : r + 1] for r in range(4)]
        item = jnp.concatenate(item * 4, axis=0)
        begin = HEAD + 32 * t
        inside = (lane >= begin) & (lane < begin + 32)
        for j in range(4):
            moved = pltpu.roll(item, (begin - 32 * j) % LANES, 1)
            out = jnp.where(inside & ((row >> 2) == j), moved, out)
    for z in range(DOM):
        out_ref[z] = out


def join_kernel(place_ref, mine_ref, came_ref, out_ref):
    row = mine_ref[...]
    row = jnp.concatenate([row[:, :BODY], row[:, BODY:] + came_ref[place_ref[SENDER]]], axis=1)
    for y in range(NY):
        out_ref[y] = row


def fill_edges(worker, wire_ref, edge_ref, table_ref, list_ref):
    wire = wire_ref[:, :, BODY:WIDE]
    shape = (HALF, SHARD, LANES)
    group = lax.broadcasted_iota(jnp.int32, shape, 2) >> 5
    kept = group == (lax.broadcasted_iota(jnp.int32, shape, 1) >> 2)
    turned = [
        pltpu.roll(wire.reshape(HALF * SHARD, LANES), (32 * d - HEAD) % LANES, 1).reshape(shape)
        for d in range(4)
    ]
    for t in range(3):
        item = turned[-t % 4]
        for j in range(1, 4):
            item = jnp.where(group == j, turned[(j - t) % 4], item)
        item = jnp.where(kept, item, 0.0)
        item = item[:, 0:8, :] + item[:, 8:16, :]
        list_ref[:, 4 * t : 4 * t + 4, :] = item[:, 0:4, :] + item[:, 4:8, :]
    rows = lax.broadcasted_iota(jnp.int32, (LANES, SLOTS), 0).astype(jnp.float32).astype(jnp.bfloat16)
    eight = lax.broadcasted_iota(jnp.int32, (8, SLOTS), 0)
    one, zero = jnp.bfloat16(1.0), jnp.bfloat16(0.0)

    def block(b, carry):
        lists = list_ref[b].astype(jnp.int32)
        src, dst, uses = (
            jnp.concatenate([lists[4 * t + r : 4 * t + r + 1] for r in range(4)], axis=1)
            for t in range(3)
        )
        src = src - worker * SHARD
        mine = (src >= 0) & (src < SHARD)
        high = dst >> 7
        code = jnp.where(mine, (high << 4) + src, -1).astype(jnp.float32).astype(jnp.bfloat16)
        low = (dst & 127).astype(jnp.float32).astype(jnp.bfloat16)
        at_pair = jnp.where(code == rows, one, zero)
        at_low = jnp.where(low == rows, one, zero)
        here = high == eight
        used = jnp.concatenate(
            [
                jnp.where(here, (uses & 255).astype(jnp.float32), 0.0),
                jnp.where(here, (uses >> 8).astype(jnp.float32), 0.0),
            ],
            axis=0,
        ).astype(jnp.bfloat16)
        both = jnp.concatenate([at_pair, used], axis=0)
        both = lax.dot_general(both, at_low, NT, preferred_element_type=jnp.float32)
        edge_ref[b] = both[0:LANES].reshape(8, SHARD, LANES)
        table_ref[b] = both[LANES : LANES + 8] + 256.0 * both[LANES + 8 : LANES + 16]
        return carry

    lax.fori_loop(0, HALF, block, 0, unroll=HALF)


def edges_kernel(place_ref, wire_ref, edge_ref, table_ref, list_ref):
    fill_edges(place_ref[WORKER], wire_ref, edge_ref, table_ref, list_ref)


def pair_kernel(place_ref, left_ref, own_ref, oth_ref, e0_ref, t0_ref, dleft_ref, keep_ref, send_ref, m_ref, e1_ref, t1_ref, list_ref):

    def rows(ref):
        return ref[...].reshape(ROWS, WIDE)

    fill_edges(place_ref[WORKER], oth_ref, e1_ref, t1_ref, list_ref)
    left = left_ref[...]
    s_own, s_oth = hi_dot(left, rows(own_ref), NT), hi_dot(left, rows(oth_ref), NT)
    first = place_ref[CORE] == 0
    s_low = jnp.where(first, s_own, s_oth)
    s_high = jnp.where(first, s_oth, s_own)
    logits = jnp.stack(
        [half[:, r * LANES : (r + 1) * LANES] for half in (s_low, s_high) for r in range(4)]
    )
    m_ref[...] = jnp.zeros_like(m_ref)

    def over_blocks(edge_ref, table_ref):
        def block(b, carry):
            counts = jnp.broadcast_to(table_ref[b][:, None, :], (8, SHARD, LANES))
            masked = jnp.where(counts > 0.0, logits, -jnp.inf)
            top = jnp.max(jnp.max(masked, axis=0), axis=1, keepdims=True)[None]
            size = jnp.exp(jnp.minimum(logits - top, 88.0))
            weights = counts * size
            total = jnp.sum(jnp.sum(weights, axis=0), axis=1, keepdims=True)[None]
            share = edge_ref[b] / (size + total)
            sums = jnp.sum(jnp.sum(share, axis=0), axis=1, keepdims=True)[None]
            m_ref[...] += sums * weights - total * share
            return carry

        lax.fori_loop(0, HALF, block, 0, unroll=HALF)

    over_blocks(e0_ref, t0_ref)
    over_blocks(e1_ref, t1_ref)
    m = m_ref[...]
    m_low = jnp.concatenate([m[r] for r in range(4)], axis=1)
    m_high = jnp.concatenate([m[r] for r in range(4, 8)], axis=1)
    m_own = jnp.where(first, m_low, m_high)
    m_oth = jnp.where(first, m_high, m_low)
    dleft = hi_dot(m_own, rows(own_ref)) + hi_dot(m_oth, rows(oth_ref))
    tail = dleft[:, BODY:]
    tail = jnp.where(
        lax.broadcasted_iota(jnp.int32, (8, LANES), 1) < HEAD, tail[0:8], pltpu.roll(tail[8:16], HEAD, 1)
    )
    dleft = [dleft[:, r * LANES : (r + 1) * LANES] for r in range(3)] + [tail]
    dleft = jnp.concatenate(dleft, axis=0)
    for z in range(DOM):
        dleft_ref[z] = dleft
    for ref, half in ((keep_ref, m_own), (send_ref, m_oth)):
        for k in range(NX):
            ref[k] = half[:, k * LANES : (k + 1) * LANES]
            ref[NX + k] = left[:, k * LANES : (k + 1) * LANES]


def relay_kernel(place_ref, keep_ref, came_ref, *out_refs):
    for k, out_ref in enumerate(out_refs):
        at = lax.rem(place_ref[AT_X] + k, NX)
        for c, ref in enumerate((keep_ref, came_ref)):
            out_ref[c, 0] = ref[at]
            for r in range(4):
                out_ref[c, 1 + r] = ref[NX + r]


def right_kernel(m0_ref, m1_ref, m2_ref, m3_ref, out_ref):
    refs = [(ref, c) for ref in (m0_ref, m1_ref, m2_ref, m3_ref) for c in range(NC)]
    mix = jnp.concatenate([ref[c, 0] for ref, c in refs], axis=0)
    left = [jnp.concatenate([ref[c, 1 + r] for ref, c in refs], axis=0) for r in range(4)]
    grads = hi_dot(mix, jnp.concatenate(left, axis=1), TN)
    out_ref[...] = grads.reshape(NY, SHARD, WIDE)


def finish_kernel(place_ref, emb_ref, ada_ref, right_ref, back_ref, emb_out, ada_out):
    back = back_ref[place_ref[TARGET]]
    tail = back[3 * SHARD :]
    tail = jnp.concatenate([tail, pltpu.roll(tail, LANES - HEAD, 1)], axis=0)
    back = jnp.concatenate([back[r * SHARD : (r + 1) * SHARD] for r in range(3)] + [tail], axis=1)
    grads = back
    for y in range(NY):
        grads = grads + right_ref[y]
    grads = grads[:, 0:D]
    eye = lax.broadcasted_iota(jnp.int32, (SHARD, SHARD), 0)
    eye = eye == lax.broadcasted_iota(jnp.int32, (SHARD, SHARD), 1)
    column = jnp.sum(jnp.where(eye, ada_ref[...], 0.0), axis=1, keepdims=True)
    column = column + jnp.sum(grads * grads, axis=1, keepdims=True) / D
    ada_out[...] = jnp.sum(jnp.where(eye, column, 0.0), axis=0, keepdims=True)
    emb_out[...] = emb_ref[...] - learn_rate * grads / (jnp.sqrt(column) + epsilon)


def swap_core(piece):
    return lax.ppermute(piece, "c", [(0, 1), (1, 0)])


def exchange(pieces, axis):
    return lax.all_to_all(pieces, axis, 0, 0)


def body(embeddings, adagrad, plan, src_ids, dst_ids, neg_ids, counts):
    part = lax.axis_index("dom")
    core = lax.axis_index("c")
    at_x = lax.axis_index("x")
    worker = (lax.axis_index("y") * NX + at_x) * NC + core
    number = jnp.arange(DOM, dtype=jnp.int32)
    sender = jnp.sum(jnp.where(plan == part, number, 0))
    target = jnp.sum(jnp.where(number == part, plan, 0))
    place = jnp.stack([worker, core, at_x, sender, target]).astype(jnp.int32)

    ids = jnp.concatenate([src_ids[0], dst_ids[0], neg_ids[0]], axis=0)
    left, mine, lists = call(
        pack_kernel,
        (f32(LEFT, WIDE), f32(SHARD, WIDE), f32(DOM, SHARD, LANES)),
        "svv",
        name="pack",
    )(counts[0], embeddings, ids)

    left = lax.all_gather(left, "dom", axis=0, tiled=True)
    left = lax.dynamic_slice_in_dim(left, sender * LEFT, SHARD, 0)
    near = call(join_kernel, f32(NY, SHARD, WIDE), "svv", name="join")(place, mine, exchange(lists, "dom"))
    near = exchange(near, "y").reshape(NY * SHARD, WIDE)
    near = exchange(jnp.broadcast_to(near, (NX, NY * SHARD, WIDE)), "x")
    far = swap_core(near)
    near, far = near.reshape(HALF, SHARD, WIDE), far.reshape(HALF, SHARD, WIDE)

    scratch = [vmem(HALF, 8, SHARD, LANES), vmem(HALF, 8, LANES), vmem(HALF, 12, LANES)]
    edges = call(
        edges_kernel,
        (f32(HALF, 8, SHARD, LANES), f32(HALF, 8, LANES)),
        "sv",
        scratch=scratch[2:],
        name="edges",
    )(place, near)
    dleft, keep, send = call(
        pair_kernel,
        (f32(DOM, BACK, LANES), f32(8, SHARD, LANES), f32(8, SHARD, LANES)),
        "svvvvv",
        scratch=[vmem(8, SHARD, LANES)] + scratch,
        name="pair",
    )(place, left, near, far, *edges)

    back = exchange(dleft, "dom")
    messages = call(relay_kernel, (f32(NC, 5, SHARD, LANES),) * NX, "svv", name="relay")(
        place, keep, swap_core(send)
    )
    messages = [messages[0]] + [
        lax.ppermute(messages[k], "x", [(i, (i + k) % NX) for i in range(NX)]) for k in range(1, NX)
    ]
    right = call(right_kernel, f32(NY, SHARD, WIDE), "vvvv", name="right")(*messages)
    right, back = lax.optimization_barrier((right, back))
    right = exchange(right, "y")
    new_embeddings, new_adagrad = call(
        finish_kernel, (f32(SHARD, D), f32(1, SHARD)), "svvvv", name="finish"
    )(place, embeddings, adagrad[None], right, back)
    return (new_embeddings, new_adagrad[0])


def solution(mesh):
    axes = ("dom", "y", "x", "c")
    grid = Mesh(mesh.devices.reshape(DOM, NY, NX, NC), axes)
    edge = P("dom", ("y", "x", "c"), None)
    in_specs = (P(axes, None), P(axes), P(), edge, edge, edge, P("dom", ("y", "x", "c")))
    out_specs = (P(axes, None), P(axes))
    return jax.shard_map(body, mesh=grid, in_specs=in_specs, out_specs=out_specs, check_vma=False)
```

time: 174 us -> 138 us (0.79)
  the two profiles are of different devices: /device:TPU:64 before, /device:TPU:6 now
where the time goes in v2:
time: 138 us; the launch traced here: 137 us
  blocking collectives  48.4 us (35%)
  starting transfers between devices  33.7 us (24%)
  waiting for transfers between devices  19.5 us (14%)
  between operations  15.4 us (11%)
  Pallas kernels  14.6 us (11%)
  local copies, waits for them, and re-layouts  2.97 us (2%)
  other arithmetic  2.09 us (2%)
    all_to_all x3, blocking collectives, exchange(): return lax.all_to_all(pieces, axis, 0, 0)  48.4 us
    all_to_all x2, starting transfers between devices, exchange(): return lax.all_to_all(pieces, axis, 0, 0)  21.2 us
    all_to_all x2, waiting for transfers between devices, exchange(): return lax.all_to_all(pieces, axis, 0, 0)  9.25 us
    pallas_call x1, Pallas kernels, body(): call(pair_kernel, (f32(DOM, BACK, LANES), f32(8, SHARD, LANES), f32(8, SH...  8.67 us
    ppermute x3, starting transfers between devices, body(): lax.ppermute(messages[k], 'x', [(i, (i + k) % NX) for i in range(NX)])  8.64 us
    ppermute x3, waiting for transfers between devices, body(): lax.ppermute(messages[k], 'x', [(i, (i + k) % NX) for i in range(NX)])  5.61 us
    ppermute x2, starting transfers between devices, swap_core(): return lax.ppermute(piece, 'c', [(0, 1), (1, 0)])  3.83 us
    all_gather x1, waiting for transfers between devices, body(): left = lax.all_gather(left, 'dom', axis=0, tiled=True)  3.42 us
  transfers between devices with their start and end apart: 8, of which 5 were waited for; matrix products, arithmetic and copies ran while one was open for 3% of the time, Pallas kernels for 3%

profile of v2, /device:TPU:6, one launch (start us, length us, event | category | flops | bytes accessed | tf_op | source)
XLA Modules:
  0.0 136.7 jit_solution(16021211451759599918)
XLA Ops:
  7.9 0.7 pad_add_fusion.ids_ref
  8.6 0.7 copy-done
  9.3 1.0 pack.1
  10.4 15.2 %all-to-all-start = ((f32[12,16,128]{2,1,0:T(8,128)}), f32[12,16,128]{2,1,0:T(8,128)S(1)}, u32[]{:S(2)}, u32[]{:S(2)}) async-start(f32[12,16,128]{2,1,0:T(8,128)} %get-tuple-element.20), calls=%async_computation | async-start | bytes 196608 | tf_op jit(solution)/shard_map/all_to_all | solution.py:252
  25.6 1.4 fusion.1
  27.0 1.3 stack.23.place_ref
  28.3 9.2 %all-to-all-done.came_ref = f32[12,16,128]{2,1,0:T(8,128)S(1)} async-done(((f32[12,16,128]{2,1,0:T(8,128)}), f32[12,16,128]{2,1,0:T(8,128)S(1)}, u32[]{:S(2)}, u32[]{:S(2)}) %all-to-all-start) | async-done | bytes 98336 | tf_op jit(solution)/shard_map/all_to_all | solution.py:252
  38.1 17.4 %all_to_all.25 = f32[8,16,512]{2,1,0:T(8,128)S(1)} all-to-all(f32[8,16,512]{2,1,0:T(8,128)S(1)} %join.1), channel_id=1, replica_groups=mesh['dom'=12,'y'=8,'x'=4,'c'=2] {'y'}, dimensions={0} | all-to-all | bytes 524288 | tf_op jit(solution)/shard_map/all_to_all | solution.py:252
  55.6 14.1 %all_to_all.26 = f32[4,128,512]{2,1,0:T(8,128)S(1)} all-to-all(f32[4,128,512]{2,1,0:T(8,128)S(1)} %broadcast_in_dim.13), channel_id=1, replica_groups=mesh['dom'=12,'y'=8,'x'=4,'c'=2] {'x'}, dimensions={0} | all-to-all | bytes 2097152 | tf_op jit(solution)/shard_map/all_to_all | solution.py:252
  69.7 1.9 %collective-permute-start = (f32[4,128,512]{2,1,0:T(8,128)S(1)}, f32[4,128,512]{2,1,0:T(8,128)}, u32[]{:S(2)}, u32[]{:S(2)}) collective-permute-start(f32[4,128,512]{2,1,0:T(8,128)S(1)} %all_to_all.26), channel_id=1, source_target_pairs={{0,1},{1,0},{2,3},{3,2},{4,5},{5,4},{6,7},{7,6},{8,9},{9,8},{10,11... | collective-permute-start | bytes 3145736 | tf_op jit(solution)/shard_map/ppermute | solution.py:248
  72.2 2.1 %edges.1 = (f32[32,8,16,128]{3,2,1,0:T(8,128)S(1)}, f32[32,8,128]{2,1,0:T(8,128)S(1)}) custom-call(s32[5]{0:T(128)S(1)} %stack.23.place_ref, f32[32,16,512]{2,1,0:T(8,128)S(1)} %bitcast.15), custom_call_target="tpu_custom_call" | custom-call | tf_op jit(solution)/shard_map/edges/pallas_call | solution.py:282
  74.3 3.4 %all-gather.2.cloned.1.call-done = f32[768,512]{1,0:T(8,128)} async-done(((f32[64,512]{1,0:T(8,128)}), f32[768,512]{1,0:T(8,128)}) %all-gather.2.cloned.1.call-update) | async-done | bytes 1572880 | tf_op jit(solution)/shard_map/all_gather | solution.py:273
  77.7 0.8 constant_dynamic-slice_fusion.left_ref
  78.5 8.7 %pair.1 = (f32[12,56,128]{2,1,0:T(8,128)}, f32[8,16,128]{2,1,0:T(8,128)S(1)}, f32[8,16,128]{2,1,0:T(8,128)S(1)}) custom-call(s32[5]{0:T(128)S(1)} %stack.23.place_ref, f32[16,512]{1,0:T(8,128)S(1)} %constant_dynamic-slice_fusion.left_ref, f32[32,16,512]{2,1,0:T(8,128)S(1)} %bitcast.16, f32[32,16,512]{2,1,0:T(8,128)} %bitcast.12.oth_ref, ...), custom_call_target="tpu_custom_call" | custom-call | tf_op jit(solution)/shard_map/pair/pallas_call | solution.py:289
  87.1 6.0 %all-to-all-start.3 = ((f32[12,56,128]{2,1,0:T(8,128)}), f32[12,56,128]{2,1,0:T(8,128)S(1)}, u32[]{:S(2)}, u32[]{:S(2)}) async-start(f32[12,56,128]{2,1,0:T(8,128)} %get-tuple-element.29), calls=%async_computation.3 | async-start | bytes 688128 | tf_op jit(solution)/shard_map/all_to_all | solution.py:252
  93.2 1.9 %collective-permute-start.1 = (f32[8,16,128]{2,1,0:T(8,128)S(1)}, f32[8,16,128]{2,1,0:T(8,128)S(1)}, u32[]{:S(2)}, u32[]{:S(2)}) collective-permute-start(f32[8,16,128]{2,1,0:T(8,128)S(1)} %get-tuple-element.24), channel_id=1, source_target_pairs={{0,1},{1,0},{2,3},{3,2},{4,5},{5,4},{6,7},{7,6},{8,9},{9,8},{10,11... | collective-permute-start | bytes 196616 | tf_op jit(solution)/shard_map/ppermute | solution.py:248
  95.1 1.2 collective-permute-done.1.came_ref
  96.9 2.4 %collective-permute-start.2 = (f32[2,5,16,128]{3,2,1,0:T(8,128)S(1)}, f32[2,5,16,128]{3,2,1,0:T(8,128)S(1)}, u32[]{:S(2)}, u32[]{:S(2)}) collective-permute-start(f32[2,5,16,128]{3,2,1,0:T(8,128)S(1)} %get-tuple-element.26), channel_id=1, source_target_pairs={{0,2},{2,4},{4,6},{6,0},{1,3},{3,5},{5,7},{7,1},{8,10},{10,12},{12... | collective-permute-start | bytes 245768 | tf_op jit(solution)/shard_map/ppermute | solution.py:302
  99.3 4.3 %collective-permute-start.3 = (f32[2,5,16,128]{3,2,1,0:T(8,128)S(1)}, f32[2,5,16,128]{3,2,1,0:T(8,128)S(1)}, u32[]{:S(2)}, u32[]{:S(2)}) collective-permute-start(f32[2,5,16,128]{3,2,1,0:T(8,128)S(1)} %get-tuple-element.27), channel_id=1, source_target_pairs={{0,4},{2,6},{4,0},{6,2},{1,5},{3,7},{5,1},{7,3},{8,12},{10,14},{12... | collective-permute-start | bytes 245768 | tf_op jit(solution)/shard_map/ppermute | solution.py:302
  103.6 1.9 %collective-permute-start.4 = (f32[2,5,16,128]{3,2,1,0:T(8,128)S(1)}, f32[2,5,16,128]{3,2,1,0:T(8,128)S(1)}, u32[]{:S(2)}, u32[]{:S(2)}) collective-permute-start(f32[2,5,16,128]{3,2,1,0:T(8,128)S(1)} %get-tuple-element.28), channel_id=1, source_target_pairs={{0,6},{2,0},{4,2},{6,4},{1,7},{3,1},{5,3},{7,5},{8,14},{10,8},{12,... | collective-permute-start | bytes 245768 | tf_op jit(solution)/shard_map/ppermute | solution.py:302
  105.6 1.6 %collective-permute-done.3.m2_ref = f32[2,5,16,128]{3,2,1,0:T(8,128)S(1)} collective-permute-done((f32[2,5,16,128]{3,2,1,0:T(8,128)S(1)}, f32[2,5,16,128]{3,2,1,0:T(8,128)S(1)}, u32[]{:S(2)}, u32[]{:S(2)}) %collective-permute-start.3) | collective-permute-done | bytes 81952 | tf_op jit(solution)/shard_map/ppermute | solution.py:302
  107.2 4.0 %collective-permute-done.4.m3_ref = f32[2,5,16,128]{3,2,1,0:T(8,128)S(1)} collective-permute-done((f32[2,5,16,128]{3,2,1,0:T(8,128)S(1)}, f32[2,5,16,128]{3,2,1,0:T(8,128)S(1)}, u32[]{:S(2)}, u32[]{:S(2)}) %collective-permute-start.4) | collective-permute-done | bytes 81952 | tf_op jit(solution)/shard_map/ppermute | solution.py:302
  111.6 17.0 %all_to_all.27.right_ref = f32[8,16,512]{2,1,0:T(8,128)S(1)} all-to-all(f32[8,16,512]{2,1,0:T(8,128)S(1)} %right.1), channel_id=1, replica_groups=mesh['dom'=12,'y'=8,'x'=4,'c'=2] {'y'}, dimensions={0} | all-to-all | bytes 524288 | tf_op jit(solution)/shard_map/all_to_all | solution.py:252
  128.6 1.3 finish.1
  (14 shorter events, 1.7 us)
Async XLA Ops:
  7.2 70.5 %all-gather.2.cloned.1.call-start = ((), (), s32[]{:S(2)}) async-start(), calls=%async_computation.5 | async-start | bytes 1703936 | tf_op jit(solution)/shard_map/all_gather | solution.py:273
  8.6 0.8 copy-start
  10.4 27.1 %all-to-all-start = ((f32[12,16,128]{2,1,0:T(8,128)}), f32[12,16,128]{2,1,0:T(8,128)S(1)}, u32[]{:S(2)}, u32[]{:S(2)}) async-start(f32[12,16,128]{2,1,0:T(8,128)} %get-tuple-element.20), calls=%async_computation | async-start | bytes 196608 | tf_op jit(solution)/shard_map/all_to_all | solution.py:252
  69.7 8.8 %collective-permute-start = (f32[4,128,512]{2,1,0:T(8,128)S(1)}, f32[4,128,512]{2,1,0:T(8,128)}, u32[]{:S(2)}, u32[]{:S(2)}) collective-permute-start(f32[4,128,512]{2,1,0:T(8,128)S(1)} %all_to_all.26), channel_id=1, source_target_pairs={{0,1},{1,0},{2,3},{3,2},{4,5},{5,4},{6,7},{7,6},{8,9},{9,8},{10,11... | collective-permute-start | bytes 3145736 | tf_op jit(solution)/shard_map/ppermute | solution.py:248
  87.1 41.4 %copy-start.1 = (f32[16,400]{1,0:T(8,128)S(1)}, f32[16,400]{1,0:T(8,128)}, u32[]{:S(2)}) copy-start(f32[16,400]{1,0:T(8,128)} %emb_ref.3) | copy-start | bytes 76804
  87.1 41.4 %copy-start.2 = (f32[16]{0:T(128)S(1)}, f32[16]{0:T(128)}, u32[]{:S(2)}) copy-start(f32[16]{0:T(128)} %param.8) | copy-start | bytes 196
  87.1 24.4 %all-to-all-start.3 = ((f32[12,56,128]{2,1,0:T(8,128)}), f32[12,56,128]{2,1,0:T(8,128)S(1)}, u32[]{:S(2)}, u32[]{:S(2)}) async-start(f32[12,56,128]{2,1,0:T(8,128)} %get-tuple-element.29), calls=%async_computation.3 | async-start | bytes 688128 | tf_op jit(solution)/shard_map/all_to_all | solution.py:252
  93.2 3.1 %collective-permute-start.1 = (f32[8,16,128]{2,1,0:T(8,128)S(1)}, f32[8,16,128]{2,1,0:T(8,128)S(1)}, u32[]{:S(2)}, u32[]{:S(2)}) collective-permute-start(f32[8,16,128]{2,1,0:T(8,128)S(1)} %get-tuple-element.24), channel_id=1, source_target_pairs={{0,1},{1,0},{2,3},{3,2},{4,5},{5,4},{6,7},{7,6},{8,9},{9,8},{10,11... | collective-permute-start | bytes 196616 | tf_op jit(solution)/shard_map/ppermute | solution.py:248
  96.9 8.7 %collective-permute-start.2 = (f32[2,5,16,128]{3,2,1,0:T(8,128)S(1)}, f32[2,5,16,128]{3,2,1,0:T(8,128)S(1)}, u32[]{:S(2)}, u32[]{:S(2)}) collective-permute-start(f32[2,5,16,128]{3,2,1,0:T(8,128)S(1)} %get-tuple-element.26), channel_id=1, source_target_pairs={{0,2},{2,4},{4,6},{6,0},{1,3},{3,5},{5,7},{7,1},{8,10},{10,12},{12... | collective-permute-start | bytes 245768 | tf_op jit(solution)/shard_map/ppermute | solution.py:302
  99.3 7.8 %collective-permute-start.3 = (f32[2,5,16,128]{3,2,1,0:T(8,128)S(1)}, f32[2,5,16,128]{3,2,1,0:T(8,128)S(1)}, u32[]{:S(2)}, u32[]{:S(2)}) collective-permute-start(f32[2,5,16,128]{3,2,1,0:T(8,128)S(1)} %get-tuple-element.27), channel_id=1, source_target_pairs={{0,4},{2,6},{4,0},{6,2},{1,5},{3,7},{5,1},{7,3},{8,12},{10,14},{12... | collective-permute-start | bytes 245768 | tf_op jit(solution)/shard_map/ppermute | solution.py:302
  103.6 7.5 %collective-permute-start.4 = (f32[2,5,16,128]{3,2,1,0:T(8,128)S(1)}, f32[2,5,16,128]{3,2,1,0:T(8,128)S(1)}, u32[]{:S(2)}, u32[]{:S(2)}) collective-permute-start(f32[2,5,16,128]{3,2,1,0:T(8,128)S(1)} %get-tuple-element.28), channel_id=1, source_target_pairs={{0,6},{2,0},{4,2},{6,4},{1,7},{3,1},{5,3},{7,5},{8,14},{10,8},{12,... | collective-permute-start | bytes 245768 | tf_op jit(solution)/shard_map/ppermute | solution.py:302
Sparse Core Ops, SparseCore 0:
  10.5 67.1 all-gather.1

commit v3 on v2

--- a/solution.py
+++ b/solution.py
@@ -22,20 +22,19 @@
 NN = (((1,), (0,)), ((), ()))
 NT = (((1,), (1,)), ((), ()))
 TN = (((0,), (0,)), ((), ()))
-LEFT = 64
 BACK = 56
 BIG = 24 * 1024 * 1024
 
 
-SPACES = {"s": pltpu.SMEM, "v": pltpu.VMEM}
-WORKER, CORE, AT_X, SENDER, TARGET = range(5)
+SPACES = {"s": pltpu.SMEM, "v": pltpu.VMEM, "a": pl.ANY}
+WORKER, CORE, AT_X, PART, SENDER, TARGET = range(6)
 
 
 def whole(space=pltpu.VMEM):
     return pl.BlockSpec(memory_space=space)
 
 
-def call(kernel, out, spaces, scratch=(), name=None):
+def call(kernel, out, spaces, scratch=(), name=None, limit=BIG):
     many = isinstance(out, tuple)
     return pl.pallas_call(
         kernel,
@@ -43,7 +42,7 @@
         in_specs=[whole(SPACES[space]) for space in spaces],
         out_specs=(whole(),) * len(out) if many else whole(),
         scratch_shapes=list(scratch),
-        compiler_params=pltpu.CompilerParams(vmem_limit_bytes=BIG),
+        compiler_params=pltpu.CompilerParams(vmem_limit_bytes=limit),
         name=name,
     )
 
@@ -60,13 +59,45 @@
     return lax.dot_general(a, b, dims, precision=HI, preferred_element_type=jnp.float32)
 
 
-def pack_kernel(count_ref, emb_ref, ids_ref, left_ref, mine_ref, out_ref):
-    for ref in (left_ref, mine_ref):
-        ref[...] = jnp.zeros_like(ref)
-        ref[0:SHARD, 0:D] = emb_ref[...]
+def split(value, parts):
+    terms = []
+    for _ in range(parts):
+        terms.append(value.astype(jnp.bfloat16))
+        value = value - terms[-1].astype(jnp.float32)
+    return terms
+
+
+def thin_dot(thin, terms, dims):
+    parts, rows = len(terms), thin.shape[0]
+    thin = split(thin, parts)
+    total = None
+    for j in reversed(range(parts)):
+        stacked = jnp.concatenate(thin[: parts - j], axis=0)
+        product = lax.dot_general(stacked, terms[j], dims, preferred_element_type=jnp.float32)
+        for i in reversed(range(parts - j)):
+            piece = product[i * rows : (i + 1) * rows]
+            total = piece if total is None else total + piece
+    return total
+
+
+def pack_kernel(count_hbm, emb_hbm, src_hbm, dst_hbm, neg_hbm, out_ref, count_ref, mine_ref, emb_ref, src_ref, dst_ref, neg_ref, sems):
+    copies = [
+        pltpu.make_async_copy(count_hbm, count_ref, sems.at[0]),
+        pltpu.make_async_copy(src_hbm.at[0], src_ref, sems.at[1]),
+        pltpu.make_async_copy(dst_hbm.at[0], dst_ref, sems.at[2]),
+        pltpu.make_async_copy(neg_hbm.at[0], neg_ref, sems.at[3]),
+        pltpu.make_async_copy(emb_hbm, emb_ref, sems.at[4]),
+    ]
+    for copy in copies:
+        copy.start()
+    mine_ref[...] = jnp.zeros_like(mine_ref)
+    for copy in copies:
+        copy.wait()
+    mine_ref[:, 0:D] = emb_ref[...]
+    mine = mine_ref[...]
     slot = lax.broadcasted_iota(jnp.int32, (1, SLOTS), 1)
-    src = jnp.where(slot < count_ref[0], ids_ref[0:1], -1)
-    dst, neg = ids_ref[1:2], ids_ref[2:3]
+    src = jnp.where(slot < count_ref[...], src_ref[...], -1)
+    dst, neg = dst_ref[...], neg_ref[...]
     place = (((dst >> 4) & 1) << 9) | (((dst >> 5) & 3) << 7) | ((dst >> 7) << 4) | (dst & 15)
     high = lax.broadcasted_iota(jnp.int32, (8, SLOTS), 0)
     low = lax.broadcasted_iota(jnp.int32, (LANES, SLOTS), 0)
@@ -79,7 +110,7 @@
     )
     row = lax.broadcasted_iota(jnp.int32, (SHARD, LANES), 0)
     lane = lax.broadcasted_iota(jnp.int32, (SHARD, LANES), 1)
-    out = jnp.zeros((SHARD, LANES), jnp.float32)
+    out = mine[:, BODY:]
     for t, item in enumerate((src, place, uses)):
         if t < 2:
             item = item.astype(jnp.float32)
@@ -92,13 +123,16 @@
         for j in range(4):
             moved = pltpu.roll(item, (begin - 32 * j) % LANES, 1)
             out = jnp.where(inside & ((row >> 2) == j), moved, out)
+    out = jnp.concatenate([mine[:, :BODY], out], axis=1)
     for z in range(DOM):
         out_ref[z] = out
 
 
-def join_kernel(place_ref, mine_ref, came_ref, out_ref):
-    row = mine_ref[...]
-    row = jnp.concatenate([row[:, :BODY], row[:, BODY:] + came_ref[place_ref[SENDER]]], axis=1)
+def join_kernel(place_ref, came_ref, left_ref, out_ref):
+    came, mine = came_ref[place_ref[SENDER]], came_ref[place_ref[PART]]
+    ours = lax.broadcasted_iota(jnp.int32, (SHARD, WIDE), 1) < D
+    left_ref[...] = jnp.where(ours, came, 0.0)
+    row = jnp.where(ours, mine, came)
     for y in range(NY):
         out_ref[y] = row
 
@@ -164,7 +198,8 @@
 
     fill_edges(place_ref[WORKER], oth_ref, e1_ref, t1_ref, list_ref)
     left = left_ref[...]
-    s_own, s_oth = hi_dot(left, rows(own_ref), NT), hi_dot(left, rows(oth_ref), NT)
+    own, oth = split(rows(own_ref), 3), split(rows(oth_ref), 3)
+    s_own, s_oth = thin_dot(left, own, NT), thin_dot(left, oth, NT)
     first = place_ref[CORE] == 0
     s_low = jnp.where(first, s_own, s_oth)
     s_high = jnp.where(first, s_oth, s_own)
@@ -195,7 +230,7 @@
     m_high = jnp.concatenate([m[r] for r in range(4, 8)], axis=1)
     m_own = jnp.where(first, m_low, m_high)
     m_oth = jnp.where(first, m_high, m_low)
-    dleft = hi_dot(m_own, rows(own_ref)) + hi_dot(m_oth, rows(oth_ref))
+    dleft = thin_dot(m_own, own, NN) + thin_dot(m_oth, oth, NN)
     tail = dleft[:, BODY:]
     tail = jnp.where(
         lax.broadcasted_iota(jnp.int32, (8, LANES), 1) < HEAD, tail[0:8], pltpu.roll(tail[8:16], HEAD, 1)
@@ -260,19 +295,22 @@
     number = jnp.arange(DOM, dtype=jnp.int32)
     sender = jnp.sum(jnp.where(plan == part, number, 0))
     target = jnp.sum(jnp.where(number == part, plan, 0))
-    place = jnp.stack([worker, core, at_x, sender, target]).astype(jnp.int32)
-
-    ids = jnp.concatenate([src_ids[0], dst_ids[0], neg_ids[0]], axis=0)
-    left, mine, lists = call(
+    place = jnp.stack([worker, core, at_x, part, sender, target]).astype(jnp.int32)
+
+    listed = pltpu.VMEM((1, SLOTS), jnp.int32)
+    sent = call(
         pack_kernel,
-        (f32(LEFT, WIDE), f32(SHARD, WIDE), f32(DOM, SHARD, LANES)),
-        "svv",
+        f32(DOM, SHARD, WIDE),
+        "aaaaa",
+        scratch=[pltpu.VMEM((1, 1), jnp.int32), vmem(SHARD, WIDE), vmem(SHARD, D)]
+        + [listed, listed, listed, pltpu.SemaphoreType.DMA((5,))],
         name="pack",
-    )(counts[0], embeddings, ids)
-
-    left = lax.all_gather(left, "dom", axis=0, tiled=True)
-    left = lax.dynamic_slice_in_dim(left, sender * LEFT, SHARD, 0)
-    near = call(join_kernel, f32(NY, SHARD, WIDE), "svv", name="join")(place, mine, exchange(lists, "dom"))
+        limit=None,
+    )(counts, embeddings, src_ids, dst_ids, neg_ids)
+
+    left, near = call(join_kernel, (f32(SHARD, WIDE), f32(NY, SHARD, WIDE)), "sv", name="join")(
+        place, exchange(sent, "dom")
+    )
     near = exchange(near, "y").reshape(NY * SHARD, WIDE)
     near = exchange(jnp.broadcast_to(near, (NX, NY * SHARD, WIDE)), "x")
     far = swap_core(near)

time: 138 us -> 125 us (0.906)
  the two profiles are of different devices: /device:TPU:6 before, /device:TPU:64 now
where the time goes in v3:
time: 125 us; the launch traced here: 124 us
  blocking collectives  51.1 us (41%)
  starting transfers between devices  31.4 us (25%)
  waiting for transfers between devices  23.9 us (19%)
  Pallas kernels  13.5 us (11%)
  local copies, waits for them, and re-layouts  1.45 us (1%)
  between operations  1.39 us (1%)
  other arithmetic  1.36 us (1%)
    all_to_all x3, blocking collectives, exchange(): return lax.all_to_all(pieces, axis, 0, 0)  51.1 us
    all_to_all x2, waiting for transfers between devices, exchange(): return lax.all_to_all(pieces, axis, 0, 0)  18.6 us
    all_to_all x2, starting transfers between devices, exchange(): return lax.all_to_all(pieces, axis, 0, 0)  18.3 us
    ppermute x3, starting transfers between devices, body(): lax.ppermute(messages[k], 'x', [(i, (i + k) % NX) for i in range(NX)])  9.17 us
    pallas_call x1, Pallas kernels, body(): call(pair_kernel, (f32(DOM, BACK, LANES), f32(8, SHARD, LANES), f32(8, SH...  6.6 us
    ppermute x2, starting transfers between devices, swap_core(): return lax.ppermute(piece, 'c', [(0, 1), (1, 0)])  3.95 us
    ppermute x3, waiting for transfers between devices, body(): lax.ppermute(messages[k], 'x', [(i, (i + k) % NX) for i in range(NX)])  3.59 us
  transfers between devices with their start and end apart: 7, of which 6 were waited for; matrix products, arithmetic and copies ran while one was open for 2% of the time, Pallas kernels for 2%

profile of v3, /device:TPU:64, one launch (start us, length us, event | category | flops | bytes accessed | tf_op | source)
XLA Modules:
  0.0 124.1 jit_solution(3803240984668753441)
XLA Ops:
  1.3 2.0 %pack.1 = f32[12,16,512]{2,1,0:T(8,128)} custom-call(s32[1,1]{1,0:T(1,128)S(6)} %copy.9.count_hbm, f32[16,400]{1,0:T(8,128)} %emb_ref.1, s32[1,1,512]{2,1,0:T(1,128)} %src_hbm.1, s32[1,1,512]{2,1,0:T(1,128)} %dst_hbm.1, s32[1,1,512]{2,1,0:T(1,128)} %neg_hbm.1), custom_call_target="tpu_custom_call" | custom-call | tf_op jit(solution)/shard_map/pack/pallas_call | solution.py:301
  3.3 14.8 %all-to-all-start = ((f32[12,16,512]{2,1,0:T(8,128)}), f32[12,16,512]{2,1,0:T(8,128)S(1)}, u32[]{:S(2)}, u32[]{:S(2)}) async-start(f32[12,16,512]{2,1,0:T(8,128)} %pack.1), calls=%async_computation | async-start | bytes 786432 | tf_op jit(solution)/shard_map/all_to_all | solution.py:287
  18.1 1.4 %fusion.1 = (s32[]{:T(128)}, s32[]{:T(128)}) fusion(s32[12]{0:T(128)} %param.9, s32[]{:T(128)} %axis_index.51), kind=kLoop, calls=%fused_computation.3 | loop fusion | flops 70 | bytes 60 | tf_op jit(solution)/shard_map/reduce_sum | solution.py:297
  19.4 1.3 %stack.27.place_ref = s32[6]{0:T(128)S(1)} concatenate(s32[1]{0:T(128)} %bitcast, s32[1]{0:T(128)} %bitcast.1, s32[1]{0:T(128)} %bitcast.2, s32[1]{0:T(128)} %bitcast.3, s32[1]{0:T(128)} %bitcast.4, s32[1]{0:T(128)} %bitcast.5), dimensions={0} | concatenate | bytes 48 | tf_op jit(solution)/shard_map/stack | solution.py:298
  20.8 17.2 %all-to-all-done.came_ref = f32[12,16,512]{2,1,0:T(8,128)S(1)} async-done(((f32[12,16,512]{2,1,0:T(8,128)}), f32[12,16,512]{2,1,0:T(8,128)S(1)}, u32[]{:S(2)}, u32[]{:S(2)}) %all-to-all-start) | async-done | bytes 393248 | tf_op jit(solution)/shard_map/all_to_all | solution.py:287
  37.9 0.6 join.1
  38.5 18.9 %all_to_all.25 = f32[8,16,512]{2,1,0:T(8,128)S(1)} all-to-all(f32[8,16,512]{2,1,0:T(8,128)S(1)} %get-tuple-element.18), channel_id=1, replica_groups=mesh['dom'=12,'y'=8,'x'=4,'c'=2] {'y'}, dimensions={0} | all-to-all | bytes 524288 | tf_op jit(solution)/shard_map/all_to_all | solution.py:287
  57.5 17.6 %all_to_all.26 = f32[4,128,512]{2,1,0:T(8,128)S(1)} all-to-all(f32[4,128,512]{2,1,0:T(8,128)S(1)} %broadcast_in_dim.13), channel_id=1, replica_groups=mesh['dom'=12,'y'=8,'x'=4,'c'=2] {'x'}, dimensions={0} | all-to-all | bytes 2097152 | tf_op jit(solution)/shard_map/all_to_all | solution.py:287
  75.2 1.9 %collective-permute-start = (f32[4,128,512]{2,1,0:T(8,128)S(1)}, f32[4,128,512]{2,1,0:T(8,128)S(1)}, u32[]{:S(2)}, u32[]{:S(2)}) collective-permute-start(f32[4,128,512]{2,1,0:T(8,128)S(1)} %all_to_all.26), channel_id=1, source_target_pairs={{0,1},{1,0},{2,3},{3,2},{4,5},{5,4},{6,7},{7,6},{8,9},{9,8},{10,11... | collective-permute-start | bytes 3145736 | tf_op jit(solution)/shard_map/ppermute | solution.py:283
  77.1 2.1 %edges.1 = (f32[32,8,16,128]{3,2,1,0:T(8,128)S(1)}, f32[32,8,128]{2,1,0:T(8,128)S(1)}) custom-call(s32[6]{0:T(128)S(1)} %stack.27.place_ref, f32[32,16,512]{2,1,0:T(8,128)S(1)} %bitcast.11), custom_call_target="tpu_custom_call" | custom-call | tf_op jit(solution)/shard_map/edges/pallas_call | solution.py:320
  79.1 0.6 collective-permute-done
  79.7 6.6 %pair.1 = (f32[12,56,128]{2,1,0:T(8,128)}, f32[8,16,128]{2,1,0:T(8,128)S(1)}, f32[8,16,128]{2,1,0:T(8,128)S(1)}) custom-call(s32[6]{0:T(128)S(1)} %stack.27.place_ref, f32[16,512]{1,0:T(8,128)S(1)} %get-tuple-element.17.left_ref, f32[32,16,512]{2,1,0:T(8,128)S(1)} %bitcast.12, f32[32,16,512]{2,1,0:T(8,128)S(1)} %bitcast.13, ...), custom_call_target="tpu_custom_call" | custom-call | tf_op jit(solution)/shard_map/pair/pallas_call | solution.py:327
  86.3 3.5 %all-to-all-start.3 = ((f32[12,56,128]{2,1,0:T(8,128)}), f32[12,56,128]{2,1,0:T(8,128)S(1)}, u32[]{:S(2)}, u32[]{:S(2)}) async-start(f32[12,56,128]{2,1,0:T(8,128)} %get-tuple-element.27), calls=%async_computation.3 | async-start | bytes 688128 | tf_op jit(solution)/shard_map/all_to_all | solution.py:287
  89.8 2.0 %collective-permute-start.1 = (f32[8,16,128]{2,1,0:T(8,128)S(1)}, f32[8,16,128]{2,1,0:T(8,128)S(1)}, u32[]{:S(2)}, u32[]{:S(2)}) collective-permute-start(f32[8,16,128]{2,1,0:T(8,128)S(1)} %get-tuple-element.22), channel_id=1, source_target_pairs={{0,1},{1,0},{2,3},{3,2},{4,5},{5,4},{6,7},{7,6},{8,9},{9,8},{10,11... | collective-permute-start | bytes 196616 | tf_op jit(solution)/shard_map/ppermute | solution.py:283
  91.8 1.1 collective-permute-done.1.came_ref
  92.9 0.6 relay.1
  93.5 2.5 %collective-permute-start.2 = (f32[2,5,16,128]{3,2,1,0:T(8,128)S(1)}, f32[2,5,16,128]{3,2,1,0:T(8,128)S(1)}, u32[]{:S(2)}, u32[]{:S(2)}) collective-permute-start(f32[2,5,16,128]{3,2,1,0:T(8,128)S(1)} %get-tuple-element.24), channel_id=1, source_target_pairs={{0,2},{2,4},{4,6},{6,0},{1,3},{3,5},{5,7},{7,1},{8,10},{10,12},{12... | collective-permute-start | bytes 245768 | tf_op jit(solution)/shard_map/ppermute | solution.py:340
  96.0 4.0 %collective-permute-start.3 = (f32[2,5,16,128]{3,2,1,0:T(8,128)S(1)}, f32[2,5,16,128]{3,2,1,0:T(8,128)S(1)}, u32[]{:S(2)}, u32[]{:S(2)}) collective-permute-start(f32[2,5,16,128]{3,2,1,0:T(8,128)S(1)} %get-tuple-element.25), channel_id=1, source_target_pairs={{0,4},{2,6},{4,0},{6,2},{1,5},{3,7},{5,1},{7,3},{8,12},{10,14},{12... | collective-permute-start | bytes 245768 | tf_op jit(solution)/shard_map/ppermute | solution.py:340
  100.0 2.7 %collective-permute-start.4 = (f32[2,5,16,128]{3,2,1,0:T(8,128)S(1)}, f32[2,5,16,128]{3,2,1,0:T(8,128)S(1)}, u32[]{:S(2)}, u32[]{:S(2)}) collective-permute-start(f32[2,5,16,128]{3,2,1,0:T(8,128)S(1)} %get-tuple-element.26), channel_id=1, source_target_pairs={{0,6},{2,0},{4,2},{6,4},{1,7},{3,1},{5,3},{7,5},{8,14},{10,8},{12,... | collective-permute-start | bytes 245768 | tf_op jit(solution)/shard_map/ppermute | solution.py:340
  102.7 1.1 collective-permute-done.3.m2_ref
  103.8 2.5 %collective-permute-done.4.m3_ref = f32[2,5,16,128]{3,2,1,0:T(8,128)S(1)} collective-permute-done((f32[2,5,16,128]{3,2,1,0:T(8,128)S(1)}, f32[2,5,16,128]{3,2,1,0:T(8,128)S(1)}, u32[]{:S(2)}, u32[]{:S(2)}) %collective-permute-start.4) | collective-permute-done | bytes 81952 | tf_op jit(solution)/shard_map/ppermute | solution.py:340
  106.7 1.4 %all-to-all-done.3.back_ref = f32[12,56,128]{2,1,0:T(8,128)S(1)} async-done(((f32[12,56,128]{2,1,0:T(8,128)}), f32[12,56,128]{2,1,0:T(8,128)S(1)}, u32[]{:S(2)}, u32[]{:S(2)}) %all-to-all-start.3) | async-done | bytes 344096 | tf_op jit(solution)/shard_map/all_to_all | solution.py:287
  108.2 14.6 %all_to_all.27.right_ref = f32[8,16,512]{2,1,0:T(8,128)S(1)} all-to-all(f32[8,16,512]{2,1,0:T(8,128)S(1)} %right.1), channel_id=1, replica_groups=mesh['dom'=12,'y'=8,'x'=4,'c'=2] {'y'}, dimensions={0} | all-to-all | bytes 524288 | tf_op jit(solution)/shard_map/all_to_all | solution.py:287
  122.7 1.3 %finish.1 = (f32[16,400]{1,0:T(8,128)}, f32[1,16]{1,0:T(1,128)}) custom-call(s32[6]{0:T(128)S(1)} %stack.27.place_ref, f32[16,400]{1,0:T(8,128)S(1)} %copy-done, f32[1,16]{1,0:T(1,128)S(1)} %bitcast.14, f32[8,16,512]{2,1,0:T(8,128)S(1)} %all_to_all.27.right_ref, f32[12,56,128]{2,1,0:T(8,128)S(1)} %all-to-all-done.3.back_ref), custom_call_target="tpu_custom_call" | custom-call | tf_op jit(solution)/shard_map/finish/pallas_call | solution.py:345
  (7 shorter events, 0.5 us)
Async XLA Ops:
  3.3 34.6 %all-to-all-start = ((f32[12,16,512]{2,1,0:T(8,128)}), f32[12,16,512]{2,1,0:T(8,128)S(1)}, u32[]{:S(2)}, u32[]{:S(2)}) async-start(f32[12,16,512]{2,1,0:T(8,128)} %pack.1), calls=%async_computation | async-start | bytes 786432 | tf_op jit(solution)/shard_map/all_to_all | solution.py:287
  75.2 4.5 %collective-permute-start = (f32[4,128,512]{2,1,0:T(8,128)S(1)}, f32[4,128,512]{2,1,0:T(8,128)S(1)}, u32[]{:S(2)}, u32[]{:S(2)}) collective-permute-start(f32[4,128,512]{2,1,0:T(8,128)S(1)} %all_to_all.26), channel_id=1, source_target_pairs={{0,1},{1,0},{2,3},{3,2},{4,5},{5,4},{6,7},{7,6},{8,9},{9,8},{10,11... | collective-permute-start | bytes 3145736 | tf_op jit(solution)/shard_map/ppermute | solution.py:283
  79.7 43.0 %copy-start = (f32[16,400]{1,0:T(8,128)S(1)}, f32[16,400]{1,0:T(8,128)}, u32[]{:S(2)}) copy-start(f32[16,400]{1,0:T(8,128)} %emb_ref.1) | copy-start | bytes 76804
  79.7 43.0 %copy-start.1 = (f32[16]{0:T(128)S(1)}, f32[16]{0:T(128)}, u32[]{:S(2)}) copy-start(f32[16]{0:T(128)} %param.8) | copy-start | bytes 196
  86.3 21.9 %all-to-all-start.3 = ((f32[12,56,128]{2,1,0:T(8,128)}), f32[12,56,128]{2,1,0:T(8,128)S(1)}, u32[]{:S(2)}, u32[]{:S(2)}) async-start(f32[12,56,128]{2,1,0:T(8,128)} %get-tuple-element.27), calls=%async_computation.3 | async-start | bytes 688128 | tf_op jit(solution)/shard_map/all_to_all | solution.py:287
  89.8 3.1 %collective-permute-start.1 = (f32[8,16,128]{2,1,0:T(8,128)S(1)}, f32[8,16,128]{2,1,0:T(8,128)S(1)}, u32[]{:S(2)}, u32[]{:S(2)}) collective-permute-start(f32[8,16,128]{2,1,0:T(8,128)S(1)} %get-tuple-element.22), channel_id=1, source_target_pairs={{0,1},{1,0},{2,3},{3,2},{4,5},{5,4},{6,7},{7,6},{8,9},{9,8},{10,11... | collective-permute-start | bytes 196616 | tf_op jit(solution)/shard_map/ppermute | solution.py:283
  93.5 9.2 %collective-permute-start.2 = (f32[2,5,16,128]{3,2,1,0:T(8,128)S(1)}, f32[2,5,16,128]{3,2,1,0:T(8,128)S(1)}, u32[]{:S(2)}, u32[]{:S(2)}) collective-permute-start(f32[2,5,16,128]{3,2,1,0:T(8,128)S(1)} %get-tuple-element.24), channel_id=1, source_target_pairs={{0,2},{2,4},{4,6},{6,0},{1,3},{3,5},{5,7},{7,1},{8,10},{10,12},{12... | collective-permute-start | bytes 245768 | tf_op jit(solution)/shard_map/ppermute | solution.py:340
  96.0 7.8 %collective-permute-start.3 = (f32[2,5,16,128]{3,2,1,0:T(8,128)S(1)}, f32[2,5,16,128]{3,2,1,0:T(8,128)S(1)}, u32[]{:S(2)}, u32[]{:S(2)}) collective-permute-start(f32[2,5,16,128]{3,2,1,0:T(8,128)S(1)} %get-tuple-element.25), channel_id=1, source_target_pairs={{0,4},{2,6},{4,0},{6,2},{1,5},{3,7},{5,1},{7,3},{8,12},{10,14},{12... | collective-permute-start | bytes 245768 | tf_op jit(solution)/shard_map/ppermute | solution.py:340
  100.0 6.3 %collective-permute-start.4 = (f32[2,5,16,128]{3,2,1,0:T(8,128)S(1)}, f32[2,5,16,128]{3,2,1,0:T(8,128)S(1)}, u32[]{:S(2)}, u32[]{:S(2)}) collective-permute-start(f32[2,5,16,128]{3,2,1,0:T(8,128)S(1)} %get-tuple-element.26), channel_id=1, source_target_pairs={{0,6},{2,0},{4,2},{6,4},{1,7},{3,1},{5,3},{7,5},{8,14},{10,8},{12,... | collective-permute-start | bytes 245768 | tf_op jit(solution)/shard_map/ppermute | solution.py:340

commit v4 on v3

--- a/solution.py
+++ b/solution.py
@@ -78,6 +78,19 @@
             piece = product[i * rows : (i + 1) * rows]
             total = piece if total is None else total + piece
     return total
+
+
+def narrow(value):
+    tail = value[:, BODY:]
+    lane = lax.broadcasted_iota(jnp.int32, (8, LANES), 1)
+    tail = jnp.where(lane < HEAD, tail[0:8], pltpu.roll(tail[8:16], HEAD, 1))
+    return jnp.concatenate([value[:, r * LANES : (r + 1) * LANES] for r in range(3)] + [tail], axis=0)
+
+
+def widen(value):
+    tail = value[3 * SHARD :]
+    tail = jnp.concatenate([tail, pltpu.roll(tail, LANES - HEAD, 1)], axis=0)
+    return jnp.concatenate([value[r * SHARD : (r + 1) * SHARD] for r in range(3)] + [tail], axis=1)
 
 
 def pack_kernel(count_hbm, emb_hbm, src_hbm, dst_hbm, neg_hbm, out_ref, count_ref, mine_ref, emb_ref, src_ref, dst_ref, neg_ref, sems):
@@ -102,10 +115,9 @@
     high = lax.broadcasted_iota(jnp.int32, (8, SLOTS), 0)
     low = lax.broadcasted_iota(jnp.int32, (LANES, SLOTS), 0)
     uses = lax.dot_general(
-        jnp.where((neg >> 7) == high, 1.0, 0.0),
-        jnp.where((neg & 127) == low, 1.0, 0.0),
+        jnp.where((neg >> 7) == high, 1.0, 0.0).astype(jnp.bfloat16),
+        jnp.where((neg & 127) == low, 1.0, 0.0).astype(jnp.bfloat16),
         NT,
-        precision=HI,
         preferred_element_type=jnp.float32,
     )
     row = lax.broadcasted_iota(jnp.int32, (SHARD, LANES), 0)
@@ -231,12 +243,7 @@
     m_own = jnp.where(first, m_low, m_high)
     m_oth = jnp.where(first, m_high, m_low)
     dleft = thin_dot(m_own, own, NN) + thin_dot(m_oth, oth, NN)
-    tail = dleft[:, BODY:]
-    tail = jnp.where(
-        lax.broadcasted_iota(jnp.int32, (8, LANES), 1) < HEAD, tail[0:8], pltpu.roll(tail[8:16], HEAD, 1)
-    )
-    dleft = [dleft[:, r * LANES : (r + 1) * LANES] for r in range(3)] + [tail]
-    dleft = jnp.concatenate(dleft, axis=0)
+    dleft = narrow(dleft)
     for z in range(DOM):
         dleft_ref[z] = dleft
     for ref, half in ((keep_ref, m_own), (send_ref, m_oth)):
@@ -259,18 +266,15 @@
     mix = jnp.concatenate([ref[c, 0] for ref, c in refs], axis=0)
     left = [jnp.concatenate([ref[c, 1 + r] for ref, c in refs], axis=0) for r in range(4)]
     grads = hi_dot(mix, jnp.concatenate(left, axis=1), TN)
-    out_ref[...] = grads.reshape(NY, SHARD, WIDE)
+    for y in range(NY):
+        out_ref[y] = narrow(grads[y * SHARD : (y + 1) * SHARD])
 
 
 def finish_kernel(place_ref, emb_ref, ada_ref, right_ref, back_ref, emb_out, ada_out):
-    back = back_ref[place_ref[TARGET]]
-    tail = back[3 * SHARD :]
-    tail = jnp.concatenate([tail, pltpu.roll(tail, LANES - HEAD, 1)], axis=0)
-    back = jnp.concatenate([back[r * SHARD : (r + 1) * SHARD] for r in range(3)] + [tail], axis=1)
-    grads = back
+    grads = back_ref[place_ref[TARGET]]
     for y in range(NY):
         grads = grads + right_ref[y]
-    grads = grads[:, 0:D]
+    grads = widen(grads)[:, 0:D]
     eye = lax.broadcasted_iota(jnp.int32, (SHARD, SHARD), 0)
     eye = eye == lax.broadcasted_iota(jnp.int32, (SHARD, SHARD), 1)
     column = jnp.sum(jnp.where(eye, ada_ref[...], 0.0), axis=1, keepdims=True)
@@ -339,7 +343,7 @@
     messages = [messages[0]] + [
         lax.ppermute(messages[k], "x", [(i, (i + k) % NX) for i in range(NX)]) for k in range(1, NX)
     ]
-    right = call(right_kernel, f32(NY, SHARD, WIDE), "vvvv", name="right")(*messages)
+    right = call(right_kernel, f32(NY, BACK, LANES), "vvvv", name="right")(*messages)
     right, back = lax.optimization_barrier((right, back))
     right = exchange(right, "y")
     new_embeddings, new_adagrad = call(

time: 125 us -> 124 us (level)
  transfers between devices with their start and end apart: 7 -> 7, of which waited for: 6 -> 6; matrix products, arithmetic and copies ran while one was open for 2% -> 2% of each run, Pallas kernels for 2% -> 3%
where the time goes in v4:
time: 124 us; the launch traced here: 123 us
  blocking collectives  50.4 us (41%)
  starting transfers between devices  31.4 us (25%)
  waiting for transfers between devices  23.8 us (19%)
  Pallas kernels  13.4 us (11%)
  local copies, waits for them, and re-layouts  1.45 us (1%)
  between operations  1.38 us (1%)
  other arithmetic  1.36 us (1%)
    all_to_all x3, blocking collectives, exchange(): return lax.all_to_all(pieces, axis, 0, 0)  50.4 us
    all_to_all x2, waiting for transfers between devices, exchange(): return lax.all_to_all(pieces, axis, 0, 0)  18.5 us
    all_to_all x2, starting transfers between devices, exchange(): return lax.all_to_all(pieces, axis, 0, 0)  18.3 us
    ppermute x3, starting transfers between devices, body(): lax.ppermute(messages[k], 'x', [(i, (i + k) % NX) for i in range(NX)])  9.17 us
    pallas_call x1, Pallas kernels, body(): call(pair_kernel, (f32(DOM, BACK, LANES), f32(8, SHARD, LANES), f32(8, SH...  6.6 us
    ppermute x2, starting transfers between devices, swap_core(): return lax.ppermute(piece, 'c', [(0, 1), (1, 0)])  3.95 us
    ppermute x3, waiting for transfers between devices, body(): lax.ppermute(messages[k], 'x', [(i, (i + k) % NX) for i in range(NX)])  3.59 us
  transfers between devices with their start and end apart: 7, of which 6 were waited for; matrix products, arithmetic and copies ran while one was open for 2% of the time, Pallas kernels for 3%

profile of v4, /device:TPU:64, one launch (start us, length us, event | category | flops | bytes accessed | tf_op | source)
XLA Modules:
  0.0 123.2 jit_solution(13243974204330977327)
XLA Ops:
  1.3 1.8 %pack.1 = f32[12,16,512]{2,1,0:T(8,128)} custom-call(s32[1,1]{1,0:T(1,128)S(6)} %copy.9.count_hbm, f32[16,400]{1,0:T(8,128)} %emb_ref.1, s32[1,1,512]{2,1,0:T(1,128)} %src_hbm.1, s32[1,1,512]{2,1,0:T(1,128)} %dst_hbm.1, s32[1,1,512]{2,1,0:T(1,128)} %neg_hbm.1), custom_call_target="tpu_custom_call" | custom-call | tf_op jit(solution)/shard_map/pack/pallas_call | solution.py:305
  3.1 14.8 %all-to-all-start = ((f32[12,16,512]{2,1,0:T(8,128)}), f32[12,16,512]{2,1,0:T(8,128)S(1)}, u32[]{:S(2)}, u32[]{:S(2)}) async-start(f32[12,16,512]{2,1,0:T(8,128)} %pack.1), calls=%async_computation | async-start | bytes 786432 | tf_op jit(solution)/shard_map/all_to_all | solution.py:291
  17.9 1.4 %fusion.1 = (s32[]{:T(128)}, s32[]{:T(128)}) fusion(s32[12]{0:T(128)} %param.9, s32[]{:T(128)} %axis_index.51), kind=kLoop, calls=%fused_computation.3 | loop fusion | flops 70 | bytes 60 | tf_op jit(solution)/shard_map/reduce_sum | solution.py:301
  19.3 1.3 %stack.27.place_ref = s32[6]{0:T(128)S(1)} concatenate(s32[1]{0:T(128)} %bitcast, s32[1]{0:T(128)} %bitcast.1, s32[1]{0:T(128)} %bitcast.2, s32[1]{0:T(128)} %bitcast.3, s32[1]{0:T(128)} %bitcast.4, s32[1]{0:T(128)} %bitcast.5), dimensions={0} | concatenate | bytes 48 | tf_op jit(solution)/shard_map/stack | solution.py:302
  20.6 17.2 %all-to-all-done.came_ref = f32[12,16,512]{2,1,0:T(8,128)S(1)} async-done(((f32[12,16,512]{2,1,0:T(8,128)}), f32[12,16,512]{2,1,0:T(8,128)S(1)}, u32[]{:S(2)}, u32[]{:S(2)}) %all-to-all-start) | async-done | bytes 393248 | tf_op jit(solution)/shard_map/all_to_all | solution.py:291
  37.8 0.6 join.1
  38.3 18.9 %all_to_all.25 = f32[8,16,512]{2,1,0:T(8,128)S(1)} all-to-all(f32[8,16,512]{2,1,0:T(8,128)S(1)} %get-tuple-element.18), channel_id=1, replica_groups=mesh['dom'=12,'y'=8,'x'=4,'c'=2] {'y'}, dimensions={0} | all-to-all | bytes 524288 | tf_op jit(solution)/shard_map/all_to_all | solution.py:291
  57.3 17.6 %all_to_all.26 = f32[4,128,512]{2,1,0:T(8,128)S(1)} all-to-all(f32[4,128,512]{2,1,0:T(8,128)S(1)} %broadcast_in_dim.13), channel_id=1, replica_groups=mesh['dom'=12,'y'=8,'x'=4,'c'=2] {'x'}, dimensions={0} | all-to-all | bytes 2097152 | tf_op jit(solution)/shard_map/all_to_all | solution.py:291
  75.0 1.9 %collective-permute-start = (f32[4,128,512]{2,1,0:T(8,128)S(1)}, f32[4,128,512]{2,1,0:T(8,128)S(1)}, u32[]{:S(2)}, u32[]{:S(2)}) collective-permute-start(f32[4,128,512]{2,1,0:T(8,128)S(1)} %all_to_all.26), channel_id=1, source_target_pairs={{0,1},{1,0},{2,3},{3,2},{4,5},{5,4},{6,7},{7,6},{8,9},{9,8},{10,11... | collective-permute-start | bytes 3145736 | tf_op jit(solution)/shard_map/ppermute | solution.py:287
  76.9 2.1 %edges.1 = (f32[32,8,16,128]{3,2,1,0:T(8,128)S(1)}, f32[32,8,128]{2,1,0:T(8,128)S(1)}) custom-call(s32[6]{0:T(128)S(1)} %stack.27.place_ref, f32[32,16,512]{2,1,0:T(8,128)S(1)} %bitcast.11), custom_call_target="tpu_custom_call" | custom-call | tf_op jit(solution)/shard_map/edges/pallas_call | solution.py:324
  79.0 0.6 collective-permute-done
  79.5 6.6 %pair.1 = (f32[12,56,128]{2,1,0:T(8,128)}, f32[8,16,128]{2,1,0:T(8,128)S(1)}, f32[8,16,128]{2,1,0:T(8,128)S(1)}) custom-call(s32[6]{0:T(128)S(1)} %stack.27.place_ref, f32[16,512]{1,0:T(8,128)S(1)} %get-tuple-element.17.left_ref, f32[32,16,512]{2,1,0:T(8,128)S(1)} %bitcast.12, f32[32,16,512]{2,1,0:T(8,128)S(1)} %bitcast.13, ...), custom_call_target="tpu_custom_call" | custom-call | tf_op jit(solution)/shard_map/pair/pallas_call | solution.py:331
  86.1 3.5 %all-to-all-start.3 = ((f32[12,56,128]{2,1,0:T(8,128)}), f32[12,56,128]{2,1,0:T(8,128)S(1)}, u32[]{:S(2)}, u32[]{:S(2)}) async-start(f32[12,56,128]{2,1,0:T(8,128)} %get-tuple-element.27), calls=%async_computation.3 | async-start | bytes 688128 | tf_op jit(solution)/shard_map/all_to_all | solution.py:291
  89.6 2.0 %collective-permute-start.1 = (f32[8,16,128]{2,1,0:T(8,128)S(1)}, f32[8,16,128]{2,1,0:T(8,128)S(1)}, u32[]{:S(2)}, u32[]{:S(2)}) collective-permute-start(f32[8,16,128]{2,1,0:T(8,128)S(1)} %get-tuple-element.22), channel_id=1, source_target_pairs={{0,1},{1,0},{2,3},{3,2},{4,5},{5,4},{6,7},{7,6},{8,9},{9,8},{10,11... | collective-permute-start | bytes 196616 | tf_op jit(solution)/shard_map/ppermute | solution.py:287
  91.7 1.1 collective-permute-done.1.came_ref
  92.8 0.6 relay.1
  93.3 2.5 %collective-permute-start.2 = (f32[2,5,16,128]{3,2,1,0:T(8,128)S(1)}, f32[2,5,16,128]{3,2,1,0:T(8,128)S(1)}, u32[]{:S(2)}, u32[]{:S(2)}) collective-permute-start(f32[2,5,16,128]{3,2,1,0:T(8,128)S(1)} %get-tuple-element.24), channel_id=1, source_target_pairs={{0,2},{2,4},{4,6},{6,0},{1,3},{3,5},{5,7},{7,1},{8,10},{10,12},{12... | collective-permute-start | bytes 245768 | tf_op jit(solution)/shard_map/ppermute | solution.py:344
  95.8 4.0 %collective-permute-start.3 = (f32[2,5,16,128]{3,2,1,0:T(8,128)S(1)}, f32[2,5,16,128]{3,2,1,0:T(8,128)S(1)}, u32[]{:S(2)}, u32[]{:S(2)}) collective-permute-start(f32[2,5,16,128]{3,2,1,0:T(8,128)S(1)} %get-tuple-element.25), channel_id=1, source_target_pairs={{0,4},{2,6},{4,0},{6,2},{1,5},{3,7},{5,1},{7,3},{8,12},{10,14},{12... | collective-permute-start | bytes 245768 | tf_op jit(solution)/shard_map/ppermute | solution.py:344
  99.8 2.7 %collective-permute-start.4 = (f32[2,5,16,128]{3,2,1,0:T(8,128)S(1)}, f32[2,5,16,128]{3,2,1,0:T(8,128)S(1)}, u32[]{:S(2)}, u32[]{:S(2)}) collective-permute-start(f32[2,5,16,128]{3,2,1,0:T(8,128)S(1)} %get-tuple-element.26), channel_id=1, source_target_pairs={{0,6},{2,0},{4,2},{6,4},{1,7},{3,1},{5,3},{7,5},{8,14},{10,8},{12,... | collective-permute-start | bytes 245768 | tf_op jit(solution)/shard_map/ppermute | solution.py:344
  102.5 1.1 collective-permute-done.3.m2_ref
  103.7 2.5 %collective-permute-done.4.m3_ref = f32[2,5,16,128]{3,2,1,0:T(8,128)S(1)} collective-permute-done((f32[2,5,16,128]{3,2,1,0:T(8,128)S(1)}, f32[2,5,16,128]{3,2,1,0:T(8,128)S(1)}, u32[]{:S(2)}, u32[]{:S(2)}) %collective-permute-start.4) | collective-permute-done | bytes 81952 | tf_op jit(solution)/shard_map/ppermute | solution.py:344
  106.6 1.4 %all-to-all-done.3.back_ref = f32[12,56,128]{2,1,0:T(8,128)S(1)} async-done(((f32[12,56,128]{2,1,0:T(8,128)}), f32[12,56,128]{2,1,0:T(8,128)S(1)}, u32[]{:S(2)}, u32[]{:S(2)}) %all-to-all-start.3) | async-done | bytes 344096 | tf_op jit(solution)/shard_map/all_to_all | solution.py:291
  108.0 13.8 %all_to_all.27.right_ref = f32[8,56,128]{2,1,0:T(8,128)S(1)} all-to-all(f32[8,56,128]{2,1,0:T(8,128)S(1)} %right.1), channel_id=1, replica_groups=mesh['dom'=12,'y'=8,'x'=4,'c'=2] {'y'}, dimensions={0} | all-to-all | bytes 458752 | tf_op jit(solution)/shard_map/all_to_all | solution.py:291
  121.9 1.3 %finish.1 = (f32[16,400]{1,0:T(8,128)}, f32[1,16]{1,0:T(1,128)}) custom-call(s32[6]{0:T(128)S(1)} %stack.27.place_ref, f32[16,400]{1,0:T(8,128)S(1)} %copy-done, f32[1,16]{1,0:T(1,128)S(1)} %bitcast.14, f32[8,56,128]{2,1,0:T(8,128)S(1)} %all_to_all.27.right_ref, f32[12,56,128]{2,1,0:T(8,128)S(1)} %all-to-all-done.3.back_ref), custom_call_target="tpu_custom_call" | custom-call | tf_op jit(solution)/shard_map/finish/pallas_call | solution.py:349
  (7 shorter events, 0.6 us)
Async XLA Ops:
  3.1 34.6 %all-to-all-start = ((f32[12,16,512]{2,1,0:T(8,128)}), f32[12,16,512]{2,1,0:T(8,128)S(1)}, u32[]{:S(2)}, u32[]{:S(2)}) async-start(f32[12,16,512]{2,1,0:T(8,128)} %pack.1), calls=%async_computation | async-start | bytes 786432 | tf_op jit(solution)/shard_map/all_to_all | solution.py:291
  75.0 4.5 %collective-permute-start = (f32[4,128,512]{2,1,0:T(8,128)S(1)}, f32[4,128,512]{2,1,0:T(8,128)S(1)}, u32[]{:S(2)}, u32[]{:S(2)}) collective-permute-start(f32[4,128,512]{2,1,0:T(8,128)S(1)} %all_to_all.26), channel_id=1, source_target_pairs={{0,1},{1,0},{2,3},{3,2},{4,5},{5,4},{6,7},{7,6},{8,9},{9,8},{10,11... | collective-permute-start | bytes 3145736 | tf_op jit(solution)/shard_map/ppermute | solution.py:287
  79.5 42.3 %copy-start = (f32[16,400]{1,0:T(8,128)S(1)}, f32[16,400]{1,0:T(8,128)}, u32[]{:S(2)}) copy-start(f32[16,400]{1,0:T(8,128)} %emb_ref.1) | copy-start | bytes 76804
  79.5 42.3 %copy-start.1 = (f32[16]{0:T(128)S(1)}, f32[16]{0:T(128)}, u32[]{:S(2)}) copy-start(f32[16]{0:T(128)} %param.8) | copy-start | bytes 196
  86.1 21.9 %all-to-all-start.3 = ((f32[12,56,128]{2,1,0:T(8,128)}), f32[12,56,128]{2,1,0:T(8,128)S(1)}, u32[]{:S(2)}, u32[]{:S(2)}) async-start(f32[12,56,128]{2,1,0:T(8,128)} %get-tuple-element.27), calls=%async_computation.3 | async-start | bytes 688128 | tf_op jit(solution)/shard_map/all_to_all | solution.py:291
  89.6 3.1 %collective-permute-start.1 = (f32[8,16,128]{2,1,0:T(8,128)S(1)}, f32[8,16,128]{2,1,0:T(8,128)S(1)}, u32[]{:S(2)}, u32[]{:S(2)}) collective-permute-start(f32[8,16,128]{2,1,0:T(8,128)S(1)} %get-tuple-element.22), channel_id=1, source_target_pairs={{0,1},{1,0},{2,3},{3,2},{4,5},{5,4},{6,7},{7,6},{8,9},{9,8},{10,11... | collective-permute-start | bytes 196616 | tf_op jit(solution)/shard_map/ppermute | solution.py:287
  93.3 9.2 %collective-permute-start.2 = (f32[2,5,16,128]{3,2,1,0:T(8,128)S(1)}, f32[2,5,16,128]{3,2,1,0:T(8,128)S(1)}, u32[]{:S(2)}, u32[]{:S(2)}) collective-permute-start(f32[2,5,16,128]{3,2,1,0:T(8,128)S(1)} %get-tuple-element.24), channel_id=1, source_target_pairs={{0,2},{2,4},{4,6},{6,0},{1,3},{3,5},{5,7},{7,1},{8,10},{10,12},{12... | collective-permute-start | bytes 245768 | tf_op jit(solution)/shard_map/ppermute | solution.py:344
  95.8 7.8 %collective-permute-start.3 = (f32[2,5,16,128]{3,2,1,0:T(8,128)S(1)}, f32[2,5,16,128]{3,2,1,0:T(8,128)S(1)}, u32[]{:S(2)}, u32[]{:S(2)}) collective-permute-start(f32[2,5,16,128]{3,2,1,0:T(8,128)S(1)} %get-tuple-element.25), channel_id=1, source_target_pairs={{0,4},{2,6},{4,0},{6,2},{1,5},{3,7},{5,1},{7,3},{8,12},{10,14},{12... | collective-permute-start | bytes 245768 | tf_op jit(solution)/shard_map/ppermute | solution.py:344
  99.8 6.3 %collective-permute-start.4 = (f32[2,5,16,128]{3,2,1,0:T(8,128)S(1)}, f32[2,5,16,128]{3,2,1,0:T(8,128)S(1)}, u32[]{:S(2)}, u32[]{:S(2)}) collective-permute-start(f32[2,5,16,128]{3,2,1,0:T(8,128)S(1)} %get-tuple-element.26), channel_id=1, source_target_pairs={{0,6},{2,0},{4,2},{6,4},{1,7},{3,1},{5,3},{7,5},{8,14},{10,8},{12,... | collective-permute-start | bytes 245768 | tf_op jit(solution)/shard_map/ppermute | solution.py:344

commit v5 on v4

--- a/solution.py
+++ b/solution.py
@@ -18,6 +18,7 @@
 ROWS = HALF * SHARD
 BODY = 384
 HEAD = D - BODY
+MARK = HEAD + 96
 HI = lax.Precision.HIGHEST
 NN = (((1,), (0,)), ((), ()))
 NT = (((1,), (1,)), ((), ()))
@@ -27,7 +28,6 @@
 
 
 SPACES = {"s": pltpu.SMEM, "v": pltpu.VMEM, "a": pl.ANY}
-WORKER, CORE, AT_X, PART, SENDER, TARGET = range(6)
 
 
 def whole(space=pltpu.VMEM):
@@ -45,6 +45,10 @@
         compiler_params=pltpu.CompilerParams(vmem_limit_bytes=limit),
         name=name,
     )
+
+
+def worker_of():
+    return (lax.axis_index("y") * NX + lax.axis_index("x")) * NC + lax.axis_index("c")
 
 
 def vmem(*shape):
@@ -93,13 +97,14 @@
     return jnp.concatenate([value[r * SHARD : (r + 1) * SHARD] for r in range(3)] + [tail], axis=1)
 
 
-def pack_kernel(count_hbm, emb_hbm, src_hbm, dst_hbm, neg_hbm, out_ref, count_ref, mine_ref, emb_ref, src_ref, dst_ref, neg_ref, sems):
+def pack_kernel(count_hbm, emb_hbm, src_hbm, dst_hbm, neg_hbm, plan_hbm, out_ref, count_ref, mine_ref, emb_ref, src_ref, dst_ref, neg_ref, plan_ref, sems):
     copies = [
         pltpu.make_async_copy(count_hbm, count_ref, sems.at[0]),
         pltpu.make_async_copy(src_hbm.at[0], src_ref, sems.at[1]),
         pltpu.make_async_copy(dst_hbm.at[0], dst_ref, sems.at[2]),
         pltpu.make_async_copy(neg_hbm.at[0], neg_ref, sems.at[3]),
         pltpu.make_async_copy(emb_hbm, emb_ref, sems.at[4]),
+        pltpu.make_async_copy(plan_hbm, plan_ref, sems.at[5]),
     ]
     for copy in copies:
         copy.start()
@@ -122,7 +127,8 @@
     )
     row = lax.broadcasted_iota(jnp.int32, (SHARD, LANES), 0)
     lane = lax.broadcasted_iota(jnp.int32, (SHARD, LANES), 1)
-    out = mine[:, BODY:]
+    target = plan_ref[lax.axis_index("dom")].astype(jnp.float32)
+    out = jnp.where(lane < MARK, mine[:, BODY:], target)
     for t, item in enumerate((src, place, uses)):
         if t < 2:
             item = item.astype(jnp.float32)
@@ -140,8 +146,13 @@
         out_ref[z] = out
 
 
-def join_kernel(place_ref, came_ref, left_ref, out_ref):
-    came, mine = came_ref[place_ref[SENDER]], came_ref[place_ref[PART]]
+def join_kernel(came_ref, left_ref, out_ref):
+    part = lax.axis_index("dom")
+    mine, came = came_ref[part], came_ref[0]
+    here = part.astype(jnp.float32)
+    for z in range(1, DOM):
+        block = came_ref[z]
+        came = jnp.where(block[:, BODY + MARK : BODY + MARK + 1] == here, block, came)
     ours = lax.broadcasted_iota(jnp.int32, (SHARD, WIDE), 1) < D
     left_ref[...] = jnp.where(ours, came, 0.0)
     row = jnp.where(ours, mine, came)
@@ -199,20 +210,21 @@
     lax.fori_loop(0, HALF, block, 0, unroll=HALF)
 
 
-def edges_kernel(place_ref, wire_ref, edge_ref, table_ref, list_ref):
-    fill_edges(place_ref[WORKER], wire_ref, edge_ref, table_ref, list_ref)
-
-
-def pair_kernel(place_ref, left_ref, own_ref, oth_ref, e0_ref, t0_ref, dleft_ref, keep_ref, send_ref, m_ref, e1_ref, t1_ref, list_ref):
+def edges_kernel(left_ref, wire_ref, edge_ref, table_ref, logit_ref, list_ref):
+    fill_edges(worker_of(), wire_ref, edge_ref, table_ref, list_ref)
+    logit_ref[...] = thin_dot(left_ref[...], split(wire_ref[...].reshape(ROWS, WIDE), 3), NT)
+
+
+def pair_kernel(left_ref, own_ref, oth_ref, e0_ref, t0_ref, s0_ref, dleft_ref, keep_ref, send_ref, m_ref, e1_ref, t1_ref, list_ref):
 
     def rows(ref):
         return ref[...].reshape(ROWS, WIDE)
 
-    fill_edges(place_ref[WORKER], oth_ref, e1_ref, t1_ref, list_ref)
+    fill_edges(worker_of(), oth_ref, e1_ref, t1_ref, list_ref)
     left = left_ref[...]
-    own, oth = split(rows(own_ref), 3), split(rows(oth_ref), 3)
-    s_own, s_oth = thin_dot(left, own, NT), thin_dot(left, oth, NT)
-    first = place_ref[CORE] == 0
+    own, oth = split(rows(own_ref), 2), split(rows(oth_ref), 3)
+    s_own, s_oth = s0_ref[...], thin_dot(left, oth, NT)
+    first = lax.axis_index("c") == 0
     s_low = jnp.where(first, s_own, s_oth)
     s_high = jnp.where(first, s_oth, s_own)
     logits = jnp.stack(
@@ -242,7 +254,7 @@
     m_high = jnp.concatenate([m[r] for r in range(4, 8)], axis=1)
     m_own = jnp.where(first, m_low, m_high)
     m_oth = jnp.where(first, m_high, m_low)
-    dleft = thin_dot(m_own, own, NN) + thin_dot(m_oth, oth, NN)
+    dleft = thin_dot(m_own, own, NN) + thin_dot(m_oth, oth[:2], NN)
     dleft = narrow(dleft)
     for z in range(DOM):
         dleft_ref[z] = dleft
@@ -252,9 +264,9 @@
             ref[NX + k] = left[:, k * LANES : (k + 1) * LANES]
 
 
-def relay_kernel(place_ref, keep_ref, came_ref, *out_refs):
+def relay_kernel(keep_ref, came_ref, *out_refs):
     for k, out_ref in enumerate(out_refs):
-        at = lax.rem(place_ref[AT_X] + k, NX)
+        at = lax.rem(lax.axis_index("x") + k, NX)
         for c, ref in enumerate((keep_ref, came_ref)):
             out_ref[c, 0] = ref[at]
             for r in range(4):
@@ -270,8 +282,12 @@
         out_ref[y] = narrow(grads[y * SHARD : (y + 1) * SHARD])
 
 
-def finish_kernel(place_ref, emb_ref, ada_ref, right_ref, back_ref, emb_out, ada_out):
-    grads = back_ref[place_ref[TARGET]]
+def finish_kernel(plan_ref, emb_ref, ada_ref, right_ref, back_ref, emb_out, ada_out):
+    here = lax.broadcasted_iota(jnp.int32, (1, DOM), 1) == lax.axis_index("dom")
+    target = jnp.sum(jnp.where(here, plan_ref[...], 0).astype(jnp.float32), axis=1, keepdims=True)
+    grads = back_ref[0]
+    for z in range(1, DOM):
+        grads = jnp.where(target == z, back_ref[z], grads)
     for y in range(NY):
         grads = grads + right_ref[y]
     grads = widen(grads)[:, 0:D]
@@ -292,28 +308,19 @@
 
 
 def body(embeddings, adagrad, plan, src_ids, dst_ids, neg_ids, counts):
-    part = lax.axis_index("dom")
-    core = lax.axis_index("c")
-    at_x = lax.axis_index("x")
-    worker = (lax.axis_index("y") * NX + at_x) * NC + core
-    number = jnp.arange(DOM, dtype=jnp.int32)
-    sender = jnp.sum(jnp.where(plan == part, number, 0))
-    target = jnp.sum(jnp.where(number == part, plan, 0))
-    place = jnp.stack([worker, core, at_x, part, sender, target]).astype(jnp.int32)
-
     listed = pltpu.VMEM((1, SLOTS), jnp.int32)
     sent = call(
         pack_kernel,
         f32(DOM, SHARD, WIDE),
-        "aaaaa",
+        "aaaaaa",
         scratch=[pltpu.VMEM((1, 1), jnp.int32), vmem(SHARD, WIDE), vmem(SHARD, D)]
-        + [listed, listed, listed, pltpu.SemaphoreType.DMA((5,))],
+        + [listed, listed, listed, pltpu.SMEM((DOM,), jnp.int32), pltpu.SemaphoreType.DMA((6,))],
         name="pack",
         limit=None,
-    )(counts, embeddings, src_ids, dst_ids, neg_ids)
-
-    left, near = call(join_kernel, (f32(SHARD, WIDE), f32(NY, SHARD, WIDE)), "sv", name="join")(
-        place, exchange(sent, "dom")
+    )(counts, embeddings, src_ids, dst_ids, neg_ids, plan)
+
+    left, near = call(join_kernel, (f32(SHARD, WIDE), f32(NY, SHARD, WIDE)), "v", name="join")(
+        exchange(sent, "dom")
     )
     near = exchange(near, "y").reshape(NY * SHARD, WIDE)
     near = exchange(jnp.broadcast_to(near, (NX, NY * SHARD, WIDE)), "x")
@@ -323,22 +330,22 @@
     scratch = [vmem(HALF, 8, SHARD, LANES), vmem(HALF, 8, LANES), vmem(HALF, 12, LANES)]
     edges = call(
         edges_kernel,
-        (f32(HALF, 8, SHARD, LANES), f32(HALF, 8, LANES)),
-        "sv",
+        (f32(HALF, 8, SHARD, LANES), f32(HALF, 8, LANES), f32(SHARD, WIDE)),
+        "vv",
         scratch=scratch[2:],
         name="edges",
-    )(place, near)
+    )(left, near)
     dleft, keep, send = call(
         pair_kernel,
         (f32(DOM, BACK, LANES), f32(8, SHARD, LANES), f32(8, SHARD, LANES)),
-        "svvvvv",
+        "vvvvvv",
         scratch=[vmem(8, SHARD, LANES)] + scratch,
         name="pair",
-    )(place, left, near, far, *edges)
+    )(left, near, far, *edges)
 
     back = exchange(dleft, "dom")
-    messages = call(relay_kernel, (f32(NC, 5, SHARD, LANES),) * NX, "svv", name="relay")(
-        place, keep, swap_core(send)
+    messages = call(relay_kernel, (f32(NC, 5, SHARD, LANES),) * NX, "vv", name="relay")(
+        keep, swap_core(send)
     )
     messages = [messages[0]] + [
         lax.ppermute(messages[k], "x", [(i, (i + k) % NX) for i in range(NX)]) for k in range(1, NX)
@@ -347,8 +354,8 @@
     right, back = lax.optimization_barrier((right, back))
     right = exchange(right, "y")
     new_embeddings, new_adagrad = call(
-        finish_kernel, (f32(SHARD, D), f32(1, SHARD)), "svvvv", name="finish"
-    )(place, embeddings, adagrad[None], right, back)
+        finish_kernel, (f32(SHARD, D), f32(1, SHARD)), "vvvvv", name="finish"
+    )(plan[None], embeddings, adagrad[None], right, back)
     return (new_embeddings, new_adagrad[0])
 
 

time: 124 us -> 122 us (0.984)
  blocking collectives: 50.4 us -> 85 us
  waiting for transfers between devices: 23.8 us -> 7.33 us
  starting transfers between devices: 31.4 us -> 16.6 us
  Pallas kernels: 13.4 us -> 10.9 us
  other arithmetic: 1.36 us -> 0 us
  local copies, waits for them, and re-layouts: 1.45 us -> 0.13 us
    all_to_all x3 -> x4, blocking collectives: 50.4 us -> 85 us  [exchange(): return lax.all_to_all(pieces, axis, 0, 0)]
    all_to_all x2 -> x1, waiting for transfers between devices: 18.5 us -> 1.93 us  [exchange(): return lax.all_to_all(pieces, axis, 0, 0)]
    all_to_all x2 -> x1, starting transfers between devices: 18.3 us -> 3.48 us  [exchange(): return lax.all_to_all(pieces, axis, 0, 0)]
    pallas_call x5, Pallas kernels: 6.36 us -> 4.79 us  [the longest x1 1.91 us: body(): call(edges_kernel, (f32(HALF, 8, SHARD, LANES), f32(HALF, 8, LANES), f32(...]
    reduce_sum x1 -> x0, other arithmetic: 1.36 us -> none  [body(): target = jnp.sum(jnp.where(number == part, plan, 0))]
    another operation x1 -> x0, local copies, waits for them, and re-layouts: 1.32 us -> none  [body(): jnp.stack([worker, core, at_x, part, sender, target]).astype(jnp.int32)]
  transfers between devices with their start and end apart: 7 -> 6, of which waited for: 6 -> 5; matrix products, arithmetic and copies ran while one was open for 2% -> 0% of each run, Pallas kernels for 3% -> 2%
where the time goes in v5:
time: 122 us; the launch traced here: 121 us
  blocking collectives  85 us (70%)
  starting transfers between devices  16.6 us (14%)
  Pallas kernels  10.9 us (9%)
  waiting for transfers between devices  7.33 us (6%)
  between operations  1.37 us (1%)
    all_to_all x4, blocking collectives, exchange(): return lax.all_to_all(pieces, axis, 0, 0)  85 us
    ppermute x3, starting transfers between devices, body(): lax.ppermute(messages[k], 'x', [(i, (i + k) % NX) for i in range(NX)])  9.17 us
    pallas_call x1, Pallas kernels, body(): call(pair_kernel, (f32(DOM, BACK, LANES), f32(8, SHARD, LANES), f32(8, SH...  5.64 us
    ppermute x2, starting transfers between devices, swap_core(): return lax.ppermute(piece, 'c', [(0, 1), (1, 0)])  3.95 us
    ppermute x3, waiting for transfers between devices, body(): lax.ppermute(messages[k], 'x', [(i, (i + k) % NX) for i in range(NX)])  3.59 us
    all_to_all x1, starting transfers between devices, exchange(): return lax.all_to_all(pieces, axis, 0, 0)  3.48 us
  transfers between devices with their start and end apart: 6, of which 5 were waited for; matrix products, arithmetic and copies ran while one was open for 0% of the time, Pallas kernels for 2%

profile of v5, /device:TPU:64, one launch (start us, length us, event | category | flops | bytes accessed | tf_op | source)
XLA Modules:
  0.0 121.3 jit_solution(8155974094775744941)
XLA Ops:
  1.3 1.9 %pack.1 = f32[12,16,512]{2,1,0:T(8,128)} custom-call(s32[1,1]{1,0:T(1,128)S(6)} %copy.9.count_hbm, f32[16,400]{1,0:T(8,128)} %emb_ref.1, s32[1,1,512]{2,1,0:T(1,128)} %src_hbm.1, s32[1,1,512]{2,1,0:T(1,128)} %dst_hbm.1, s32[1,1,512]{2,1,0:T(1,128)} %neg_hbm.1, s32[12]{0:T(128)} %plan_hbm.1), custom_call_target="tpu_custom_call" | custom-call | tf_op jit(solution)/shard_map/pack/pallas_call | solution.py:312
  3.1 34.6 %all_to_all.25.came_ref = f32[12,16,512]{2,1,0:T(8,128)S(1)} all-to-all(f32[12,16,512]{2,1,0:T(8,128)} %pack.1), channel_id=1, replica_groups=mesh['dom'=12,'y'=8,'x'=4,'c'=2] {'dom'}, dimensions={0} | all-to-all | bytes 786432 | tf_op jit(solution)/shard_map/all_to_all | solution.py:307
  37.8 0.1 join.1
  37.9 18.9 %all_to_all.26 = f32[8,16,512]{2,1,0:T(8,128)S(1)} all-to-all(f32[8,16,512]{2,1,0:T(8,128)S(1)} %get-tuple-element.19), channel_id=1, replica_groups=mesh['dom'=12,'y'=8,'x'=4,'c'=2] {'y'}, dimensions={0} | all-to-all | bytes 524288 | tf_op jit(solution)/shard_map/all_to_all | solution.py:307
  56.8 0.1 broadcast_in_dim.11
  56.9 17.6 %all_to_all.27 = f32[4,128,512]{2,1,0:T(8,128)S(1)} all-to-all(f32[4,128,512]{2,1,0:T(8,128)S(1)} %broadcast_in_dim.11), channel_id=1, replica_groups=mesh['dom'=12,'y'=8,'x'=4,'c'=2] {'x'}, dimensions={0} | all-to-all | bytes 2097152 | tf_op jit(solution)/shard_map/all_to_all | solution.py:307
  74.5 1.9 %collective-permute-start = (f32[4,128,512]{2,1,0:T(8,128)S(1)}, f32[4,128,512]{2,1,0:T(8,128)S(1)}, u32[]{:S(2)}, u32[]{:S(2)}) collective-permute-start(f32[4,128,512]{2,1,0:T(8,128)S(1)} %all_to_all.27), channel_id=1, source_target_pairs={{0,1},{1,0},{2,3},{3,2},{4,5},{5,4},{6,7},{7,6},{8,9},{9,8},{10,11... | collective-permute-start | bytes 3145736 | tf_op jit(solution)/shard_map/ppermute | solution.py:303
  76.5 1.9 %edges.1 = (f32[32,8,16,128]{3,2,1,0:T(8,128)S(1)}, f32[32,8,128]{2,1,0:T(8,128)S(1)}, f32[16,512]{1,0:T(8,128)S(1)}) custom-call(f32[16,512]{1,0:T(8,128)S(1)} %get-tuple-element.18.left_ref, f32[32,16,512]{2,1,0:T(8,128)S(1)} %bitcast.6), custom_call_target="tpu_custom_call" | custom-call | tf_op jit(solution)/shard_map/edges/pallas_call | solution.py:331
  78.4 0.7 collective-permute-done
  79.1 5.6 %pair.1 = (f32[12,56,128]{2,1,0:T(8,128)}, f32[8,16,128]{2,1,0:T(8,128)S(1)}, f32[8,16,128]{2,1,0:T(8,128)S(1)}) custom-call(f32[16,512]{1,0:T(8,128)S(1)} %get-tuple-element.18.left_ref, f32[32,16,512]{2,1,0:T(8,128)S(1)} %bitcast.7, f32[32,16,512]{2,1,0:T(8,128)S(1)} %bitcast.8, f32[32,8,16,128]{3,2,1,0:T(8,128)S(1)} %get-tuple-element.20.e0_ref, ...), custom_call_target="tpu_custom_call" | custom-call | tf_op jit(solution)/shard_map/pair/pallas_call | solution.py:338
  84.7 3.5 %all-to-all-start.3 = ((f32[12,56,128]{2,1,0:T(8,128)}), f32[12,56,128]{2,1,0:T(8,128)S(1)}, u32[]{:S(2)}, u32[]{:S(2)}) async-start(f32[12,56,128]{2,1,0:T(8,128)} %get-tuple-element.29), calls=%async_computation.3 | async-start | bytes 688128 | tf_op jit(solution)/shard_map/all_to_all | solution.py:307
  88.2 2.0 %collective-permute-start.1 = (f32[8,16,128]{2,1,0:T(8,128)S(1)}, f32[8,16,128]{2,1,0:T(8,128)S(1)}, u32[]{:S(2)}, u32[]{:S(2)}) collective-permute-start(f32[8,16,128]{2,1,0:T(8,128)S(1)} %get-tuple-element.24), channel_id=1, source_target_pairs={{0,1},{1,0},{2,3},{3,2},{4,5},{5,4},{6,7},{7,6},{8,9},{9,8},{10,11... | collective-permute-start | bytes 196616 | tf_op jit(solution)/shard_map/ppermute | solution.py:303
  90.3 1.1 collective-permute-done.1.came_ref
  91.4 2.5 %collective-permute-start.2 = (f32[2,5,16,128]{3,2,1,0:T(8,128)S(1)}, f32[2,5,16,128]{3,2,1,0:T(8,128)S(1)}, u32[]{:S(2)}, u32[]{:S(2)}) collective-permute-start(f32[2,5,16,128]{3,2,1,0:T(8,128)S(1)} %get-tuple-element.26), channel_id=1, source_target_pairs={{0,2},{2,4},{4,6},{6,0},{1,3},{3,5},{5,7},{7,1},{8,10},{10,12},{12... | collective-permute-start | bytes 245768 | tf_op jit(solution)/shard_map/ppermute | solution.py:351
  93.9 4.0 %collective-permute-start.3 = (f32[2,5,16,128]{3,2,1,0:T(8,128)S(1)}, f32[2,5,16,128]{3,2,1,0:T(8,128)S(1)}, u32[]{:S(2)}, u32[]{:S(2)}) collective-permute-start(f32[2,5,16,128]{3,2,1,0:T(8,128)S(1)} %get-tuple-element.27), channel_id=1, source_target_pairs={{0,4},{2,6},{4,0},{6,2},{1,5},{3,7},{5,1},{7,3},{8,12},{10,14},{12... | collective-permute-start | bytes 245768 | tf_op jit(solution)/shard_map/ppermute | solution.py:351
  97.8 2.7 %collective-permute-start.4 = (f32[2,5,16,128]{3,2,1,0:T(8,128)S(1)}, f32[2,5,16,128]{3,2,1,0:T(8,128)S(1)}, u32[]{:S(2)}, u32[]{:S(2)}) collective-permute-start(f32[2,5,16,128]{3,2,1,0:T(8,128)S(1)} %get-tuple-element.28), channel_id=1, source_target_pairs={{0,6},{2,0},{4,2},{6,4},{1,7},{3,1},{5,3},{7,5},{8,14},{10,8},{12,... | collective-permute-start | bytes 245768 | tf_op jit(solution)/shard_map/ppermute | solution.py:351
  100.6 0.0 collective-permute-done.2.m1_ref
  100.6 1.1 collective-permute-done.3.m2_ref
  101.7 2.5 %collective-permute-done.4.m3_ref = f32[2,5,16,128]{3,2,1,0:T(8,128)S(1)} collective-permute-done((f32[2,5,16,128]{3,2,1,0:T(8,128)S(1)}, f32[2,5,16,128]{3,2,1,0:T(8,128)S(1)}, u32[]{:S(2)}, u32[]{:S(2)}) %collective-permute-start.4) | collective-permute-done | bytes 81952 | tf_op jit(solution)/shard_map/ppermute | solution.py:351
  104.2 0.5 right.1
  104.7 1.9 %all-to-all-done.3.back_ref = f32[12,56,128]{2,1,0:T(8,128)S(1)} async-done(((f32[12,56,128]{2,1,0:T(8,128)}), f32[12,56,128]{2,1,0:T(8,128)S(1)}, u32[]{:S(2)}, u32[]{:S(2)}) %all-to-all-start.3) | async-done | bytes 344096 | tf_op jit(solution)/shard_map/all_to_all | solution.py:307
  106.6 13.8 %all_to_all.28.right_ref = f32[8,56,128]{2,1,0:T(8,128)S(1)} all-to-all(f32[8,56,128]{2,1,0:T(8,128)S(1)} %right.1), channel_id=1, replica_groups=mesh['dom'=12,'y'=8,'x'=4,'c'=2] {'y'}, dimensions={0} | all-to-all | bytes 458752 | tf_op jit(solution)/shard_map/all_to_all | solution.py:307
  120.4 0.0 copy-done.1
  120.5 0.9 finish.1
  (6 shorter events, 0.0 us)
Async XLA Ops:
  74.5 4.5 %collective-permute-start = (f32[4,128,512]{2,1,0:T(8,128)S(1)}, f32[4,128,512]{2,1,0:T(8,128)S(1)}, u32[]{:S(2)}, u32[]{:S(2)}) collective-permute-start(f32[4,128,512]{2,1,0:T(8,128)S(1)} %all_to_all.27), channel_id=1, source_target_pairs={{0,1},{1,0},{2,3},{3,2},{4,5},{5,4},{6,7},{7,6},{8,9},{9,8},{10,11... | collective-permute-start | bytes 3145736 | tf_op jit(solution)/shard_map/ppermute | solution.py:303
  79.1 41.4 %copy-start = (f32[16,400]{1,0:T(8,128)S(1)}, f32[16,400]{1,0:T(8,128)}, u32[]{:S(2)}) copy-start(f32[16,400]{1,0:T(8,128)} %emb_ref.1) | copy-start | bytes 76804
  79.1 41.4 %copy-start.1 = (s32[12]{0:T(128)S(1)}, s32[12]{0:T(128)}, u32[]{:S(2)}) copy-start(s32[12]{0:T(128)} %plan_hbm.1) | copy-start | bytes 148
  79.1 41.4 %copy-start.2 = (f32[16]{0:T(128)S(1)}, f32[16]{0:T(128)}, u32[]{:S(2)}) copy-start(f32[16]{0:T(128)} %param.8) | copy-start | bytes 196
  84.7 21.9 %all-to-all-start.3 = ((f32[12,56,128]{2,1,0:T(8,128)}), f32[12,56,128]{2,1,0:T(8,128)S(1)}, u32[]{:S(2)}, u32[]{:S(2)}) async-start(f32[12,56,128]{2,1,0:T(8,128)} %get-tuple-element.29), calls=%async_computation.3 | async-start | bytes 688128 | tf_op jit(solution)/shard_map/all_to_all | solution.py:307
  88.2 3.1 %collective-permute-start.1 = (f32[8,16,128]{2,1,0:T(8,128)S(1)}, f32[8,16,128]{2,1,0:T(8,128)S(1)}, u32[]{:S(2)}, u32[]{:S(2)}) collective-permute-start(f32[8,16,128]{2,1,0:T(8,128)S(1)} %get-tuple-element.24), channel_id=1, source_target_pairs={{0,1},{1,0},{2,3},{3,2},{4,5},{5,4},{6,7},{7,6},{8,9},{9,8},{10,11... | collective-permute-start | bytes 196616 | tf_op jit(solution)/shard_map/ppermute | solution.py:303
  91.4 9.2 %collective-permute-start.2 = (f32[2,5,16,128]{3,2,1,0:T(8,128)S(1)}, f32[2,5,16,128]{3,2,1,0:T(8,128)S(1)}, u32[]{:S(2)}, u32[]{:S(2)}) collective-permute-start(f32[2,5,16,128]{3,2,1,0:T(8,128)S(1)} %get-tuple-element.26), channel_id=1, source_target_pairs={{0,2},{2,4},{4,6},{6,0},{1,3},{3,5},{5,7},{7,1},{8,10},{10,12},{12... | collective-permute-start | bytes 245768 | tf_op jit(solution)/shard_map/ppermute | solution.py:351
  93.9 7.8 %collective-permute-start.3 = (f32[2,5,16,128]{3,2,1,0:T(8,128)S(1)}, f32[2,5,16,128]{3,2,1,0:T(8,128)S(1)}, u32[]{:S(2)}, u32[]{:S(2)}) collective-permute-start(f32[2,5,16,128]{3,2,1,0:T(8,128)S(1)} %get-tuple-element.27), channel_id=1, source_target_pairs={{0,4},{2,6},{4,0},{6,2},{1,5},{3,7},{5,1},{7,3},{8,12},{10,14},{12... | collective-permute-start | bytes 245768 | tf_op jit(solution)/shard_map/ppermute | solution.py:351
  97.8 6.3 %collective-permute-start.4 = (f32[2,5,16,128]{3,2,1,0:T(8,128)S(1)}, f32[2,5,16,128]{3,2,1,0:T(8,128)S(1)}, u32[]{:S(2)}, u32[]{:S(2)}) collective-permute-start(f32[2,5,16,128]{3,2,1,0:T(8,128)S(1)} %get-tuple-element.28), channel_id=1, source_target_pairs={{0,6},{2,0},{4,2},{6,4},{1,7},{3,1},{5,3},{7,5},{8,14},{10,8},{12,... | collective-permute-start | bytes 245768 | tf_op jit(solution)/shard_map/ppermute | solution.py:351

commit v6 on v5

--- a/solution.py
+++ b/solution.py
@@ -210,19 +210,21 @@
     lax.fori_loop(0, HALF, block, 0, unroll=HALF)
 
 
-def edges_kernel(left_ref, wire_ref, edge_ref, table_ref, logit_ref, list_ref):
+def edges_kernel(left_ref, wire_ref, edge_ref, table_ref, logit_ref, high_ref, low_ref, list_ref):
     fill_edges(worker_of(), wire_ref, edge_ref, table_ref, list_ref)
-    logit_ref[...] = thin_dot(left_ref[...], split(wire_ref[...].reshape(ROWS, WIDE), 3), NT)
-
-
-def pair_kernel(left_ref, own_ref, oth_ref, e0_ref, t0_ref, s0_ref, dleft_ref, keep_ref, send_ref, m_ref, e1_ref, t1_ref, list_ref):
+    terms = split(wire_ref[...].reshape(ROWS, WIDE), 3)
+    logit_ref[...] = thin_dot(left_ref[...], terms, NT)
+    high_ref[...], low_ref[...] = terms[0], terms[1]
+
+
+def pair_kernel(left_ref, oth_ref, e0_ref, t0_ref, s0_ref, high_ref, low_ref, dleft_ref, keep_ref, send_ref, m_ref, e1_ref, t1_ref, list_ref):
 
     def rows(ref):
         return ref[...].reshape(ROWS, WIDE)
 
     fill_edges(worker_of(), oth_ref, e1_ref, t1_ref, list_ref)
     left = left_ref[...]
-    own, oth = split(rows(own_ref), 2), split(rows(oth_ref), 3)
+    own, oth = [high_ref[...], low_ref[...]], split(rows(oth_ref), 3)
     s_own, s_oth = s0_ref[...], thin_dot(left, oth, NT)
     first = lax.axis_index("c") == 0
     s_low = jnp.where(first, s_own, s_oth)
@@ -330,7 +332,8 @@
     scratch = [vmem(HALF, 8, SHARD, LANES), vmem(HALF, 8, LANES), vmem(HALF, 12, LANES)]
     edges = call(
         edges_kernel,
-        (f32(HALF, 8, SHARD, LANES), f32(HALF, 8, LANES), f32(SHARD, WIDE)),
+        (f32(HALF, 8, SHARD, LANES), f32(HALF, 8, LANES), f32(SHARD, WIDE))
+        + (jax.ShapeDtypeStruct((ROWS, WIDE), jnp.bfloat16),) * 2,
         "vv",
         scratch=scratch[2:],
         name="edges",
@@ -338,10 +341,10 @@
     dleft, keep, send = call(
         pair_kernel,
         (f32(DOM, BACK, LANES), f32(8, SHARD, LANES), f32(8, SHARD, LANES)),
-        "vvvvvv",
+        "vvvvvvv",
         scratch=[vmem(8, SHARD, LANES)] + scratch,
         name="pair",
-    )(left, near, far, *edges)
+    )(left, far, *edges)
 
     back = exchange(dleft, "dom")
     messages = call(relay_kernel, (f32(NC, 5, SHARD, LANES),) * NX, "vv", name="relay")(

time: 122 us -> 122 us (level)
  no operation moved by 1% of the time
where the time goes in v6:
time: 122 us; the launch traced here: 121 us
  blocking collectives  85 us (70%)
  starting transfers between devices  16.6 us (14%)
  Pallas kernels  10.8 us (9%)
  waiting for transfers between devices  7.26 us (6%)
  between operations  1.37 us (1%)
    all_to_all x4, blocking collectives, exchange(): return lax.all_to_all(pieces, axis, 0, 0)  85 us
    ppermute x3, starting transfers between devices, body(): lax.ppermute(messages[k], 'x', [(i, (i + k) % NX) for i in range(NX)])  9.17 us
    pallas_call x1, Pallas kernels, body(): call(pair_kernel, (f32(DOM, BACK, LANES), f32(8, SHARD, LANES), f32(8, SH...  5.47 us
    ppermute x2, starting transfers between devices, swap_core(): return lax.ppermute(piece, 'c', [(0, 1), (1, 0)])  3.95 us
    ppermute x3, waiting for transfers between devices, body(): lax.ppermute(messages[k], 'x', [(i, (i + k) % NX) for i in range(NX)])  3.59 us
    all_to_all x1, starting transfers between devices, exchange(): return lax.all_to_all(pieces, axis, 0, 0)  3.48 us
  transfers between devices with their start and end apart: 6, of which 5 were waited for; matrix products, arithmetic and copies ran while one was open for 0% of the time, Pallas kernels for 2%

profile of v6, /device:TPU:64, one launch (start us, length us, event | category | flops | bytes accessed | tf_op | source)
XLA Modules:
  0.0 121.2 jit_solution(8851682951264185620)
XLA Ops:
  1.3 1.9 %pack.1 = f32[12,16,512]{2,1,0:T(8,128)} custom-call(s32[1,1]{1,0:T(1,128)S(6)} %copy.9.count_hbm, f32[16,400]{1,0:T(8,128)} %emb_ref.1, s32[1,1,512]{2,1,0:T(1,128)} %src_hbm.1, s32[1,1,512]{2,1,0:T(1,128)} %dst_hbm.1, s32[1,1,512]{2,1,0:T(1,128)} %neg_hbm.1, s32[12]{0:T(128)} %plan_hbm.1), custom_call_target="tpu_custom_call" | custom-call | tf_op jit(solution)/shard_map/pack/pallas_call | solution.py:314
  3.1 34.6 %all_to_all.25.came_ref = f32[12,16,512]{2,1,0:T(8,128)S(1)} all-to-all(f32[12,16,512]{2,1,0:T(8,128)} %pack.1), channel_id=1, replica_groups=mesh['dom'=12,'y'=8,'x'=4,'c'=2] {'dom'}, dimensions={0} | all-to-all | bytes 786432 | tf_op jit(solution)/shard_map/all_to_all | solution.py:309
  37.8 0.1 join.1
  37.9 18.9 %all_to_all.26 = f32[8,16,512]{2,1,0:T(8,128)S(1)} all-to-all(f32[8,16,512]{2,1,0:T(8,128)S(1)} %get-tuple-element.21), channel_id=1, replica_groups=mesh['dom'=12,'y'=8,'x'=4,'c'=2] {'y'}, dimensions={0} | all-to-all | bytes 524288 | tf_op jit(solution)/shard_map/all_to_all | solution.py:309
  56.8 0.1 broadcast_in_dim.11
  56.9 17.6 %all_to_all.27 = f32[4,128,512]{2,1,0:T(8,128)S(1)} all-to-all(f32[4,128,512]{2,1,0:T(8,128)S(1)} %broadcast_in_dim.11), channel_id=1, replica_groups=mesh['dom'=12,'y'=8,'x'=4,'c'=2] {'x'}, dimensions={0} | all-to-all | bytes 2097152 | tf_op jit(solution)/shard_map/all_to_all | solution.py:309
  74.5 1.9 %collective-permute-start = (f32[4,128,512]{2,1,0:T(8,128)S(1)}, f32[4,128,512]{2,1,0:T(8,128)S(1)}, u32[]{:S(2)}, u32[]{:S(2)}) collective-permute-start(f32[4,128,512]{2,1,0:T(8,128)S(1)} %all_to_all.27), channel_id=1, source_target_pairs={{0,1},{1,0},{2,3},{3,2},{4,5},{5,4},{6,7},{7,6},{8,9},{9,8},{10,11... | collective-permute-start | bytes 3145736 | tf_op jit(solution)/shard_map/ppermute | solution.py:305
  76.5 2.0 %edges.1 = (f32[32,8,16,128]{3,2,1,0:T(8,128)S(1)}, f32[32,8,128]{2,1,0:T(8,128)S(1)}, f32[16,512]{1,0:T(8,128)S(1)}, bf16[512,512]{1,0:T(8,128)(2,1)S(1)}, bf16[512,512]{1,0:T(8,128)(2,1)S(1)}) custom-call(f32[16,512]{1,0:T(8,128)S(1)} %get-tuple-element.20.left_ref, f32[32,16,512]{2,1,0:T(8,128)S(1)} %bitcast.6), custom_call_target="tpu_custom_call" | custom-call | tf_op jit(solution)/shard_map/edges/pallas_call | solution.py:333
  78.4 0.6 collective-permute-done
  79.1 5.5 %pair.1 = (f32[12,56,128]{2,1,0:T(8,128)}, f32[8,16,128]{2,1,0:T(8,128)S(1)}, f32[8,16,128]{2,1,0:T(8,128)S(1)}) custom-call(f32[16,512]{1,0:T(8,128)S(1)} %get-tuple-element.20.left_ref, f32[32,16,512]{2,1,0:T(8,128)S(1)} %bitcast.7, f32[32,8,16,128]{3,2,1,0:T(8,128)S(1)} %get-tuple-element.22.e0_ref, f32[32,8,128]{2,1,0:T(8,128)S(1)} %get-tuple-element.23.t0_ref, ...), custom_call_target="tpu_custom_call" | custom-call | tf_op jit(solution)/shard_map/pair/pallas_call | solution.py:341
  84.6 3.5 %all-to-all-start.3 = ((f32[12,56,128]{2,1,0:T(8,128)}), f32[12,56,128]{2,1,0:T(8,128)S(1)}, u32[]{:S(2)}, u32[]{:S(2)}) async-start(f32[12,56,128]{2,1,0:T(8,128)} %get-tuple-element.33), calls=%async_computation.3 | async-start | bytes 688128 | tf_op jit(solution)/shard_map/all_to_all | solution.py:309
  88.1 2.0 %collective-permute-start.1 = (f32[8,16,128]{2,1,0:T(8,128)S(1)}, f32[8,16,128]{2,1,0:T(8,128)S(1)}, u32[]{:S(2)}, u32[]{:S(2)}) collective-permute-start(f32[8,16,128]{2,1,0:T(8,128)S(1)} %get-tuple-element.28), channel_id=1, source_target_pairs={{0,1},{1,0},{2,3},{3,2},{4,5},{5,4},{6,7},{7,6},{8,9},{9,8},{10,11... | collective-permute-start | bytes 196616 | tf_op jit(solution)/shard_map/ppermute | solution.py:305
  90.1 1.1 collective-permute-done.1.came_ref
  91.2 2.5 %collective-permute-start.2 = (f32[2,5,16,128]{3,2,1,0:T(8,128)S(1)}, f32[2,5,16,128]{3,2,1,0:T(8,128)S(1)}, u32[]{:S(2)}, u32[]{:S(2)}) collective-permute-start(f32[2,5,16,128]{3,2,1,0:T(8,128)S(1)} %get-tuple-element.30), channel_id=1, source_target_pairs={{0,2},{2,4},{4,6},{6,0},{1,3},{3,5},{5,7},{7,1},{8,10},{10,12},{12... | collective-permute-start | bytes 245768 | tf_op jit(solution)/shard_map/ppermute | solution.py:354
  93.7 4.0 %collective-permute-start.3 = (f32[2,5,16,128]{3,2,1,0:T(8,128)S(1)}, f32[2,5,16,128]{3,2,1,0:T(8,128)S(1)}, u32[]{:S(2)}, u32[]{:S(2)}) collective-permute-start(f32[2,5,16,128]{3,2,1,0:T(8,128)S(1)} %get-tuple-element.31), channel_id=1, source_target_pairs={{0,4},{2,6},{4,0},{6,2},{1,5},{3,7},{5,1},{7,3},{8,12},{10,14},{12... | collective-permute-start | bytes 245768 | tf_op jit(solution)/shard_map/ppermute | solution.py:354
  97.7 2.7 %collective-permute-start.4 = (f32[2,5,16,128]{3,2,1,0:T(8,128)S(1)}, f32[2,5,16,128]{3,2,1,0:T(8,128)S(1)}, u32[]{:S(2)}, u32[]{:S(2)}) collective-permute-start(f32[2,5,16,128]{3,2,1,0:T(8,128)S(1)} %get-tuple-element.32), channel_id=1, source_target_pairs={{0,6},{2,0},{4,2},{6,4},{1,7},{3,1},{5,3},{7,5},{8,14},{10,8},{12,... | collective-permute-start | bytes 245768 | tf_op jit(solution)/shard_map/ppermute | solution.py:354
  100.4 0.0 collective-permute-done.2.m1_ref
  100.4 1.1 collective-permute-done.3.m2_ref
  101.5 2.5 %collective-permute-done.4.m3_ref = f32[2,5,16,128]{3,2,1,0:T(8,128)S(1)} collective-permute-done((f32[2,5,16,128]{3,2,1,0:T(8,128)S(1)}, f32[2,5,16,128]{3,2,1,0:T(8,128)S(1)}, u32[]{:S(2)}, u32[]{:S(2)}) %collective-permute-start.4) | collective-permute-done | bytes 81952 | tf_op jit(solution)/shard_map/ppermute | solution.py:354
  104.0 0.5 right.1
  104.5 1.9 %all-to-all-done.3.back_ref = f32[12,56,128]{2,1,0:T(8,128)S(1)} async-done(((f32[12,56,128]{2,1,0:T(8,128)}), f32[12,56,128]{2,1,0:T(8,128)S(1)}, u32[]{:S(2)}, u32[]{:S(2)}) %all-to-all-start.3) | async-done | bytes 344096 | tf_op jit(solution)/shard_map/all_to_all | solution.py:309
  106.4 13.8 %all_to_all.28.right_ref = f32[8,56,128]{2,1,0:T(8,128)S(1)} all-to-all(f32[8,56,128]{2,1,0:T(8,128)S(1)} %right.1), channel_id=1, replica_groups=mesh['dom'=12,'y'=8,'x'=4,'c'=2] {'y'}, dimensions={0} | all-to-all | bytes 458752 | tf_op jit(solution)/shard_map/all_to_all | solution.py:309
  120.3 0.0 copy-done
  120.3 0.9 finish.1
  (6 shorter events, 0.0 us)
Async XLA Ops:
  74.5 4.5 %collective-permute-start = (f32[4,128,512]{2,1,0:T(8,128)S(1)}, f32[4,128,512]{2,1,0:T(8,128)S(1)}, u32[]{:S(2)}, u32[]{:S(2)}) collective-permute-start(f32[4,128,512]{2,1,0:T(8,128)S(1)} %all_to_all.27), channel_id=1, source_target_pairs={{0,1},{1,0},{2,3},{3,2},{4,5},{5,4},{6,7},{7,6},{8,9},{9,8},{10,11... | collective-permute-start | bytes 3145736 | tf_op jit(solution)/shard_map/ppermute | solution.py:305
  79.1 41.2 %copy-start = (f32[16,400]{1,0:T(8,128)S(1)}, f32[16,400]{1,0:T(8,128)}, u32[]{:S(2)}) copy-start(f32[16,400]{1,0:T(8,128)} %emb_ref.1) | copy-start | bytes 76804
  79.1 41.2 %copy-start.1 = (s32[12]{0:T(128)S(1)}, s32[12]{0:T(128)}, u32[]{:S(2)}) copy-start(s32[12]{0:T(128)} %plan_hbm.1) | copy-start | bytes 148
  79.1 41.2 %copy-start.2 = (f32[16]{0:T(128)S(1)}, f32[16]{0:T(128)}, u32[]{:S(2)}) copy-start(f32[16]{0:T(128)} %param.8) | copy-start | bytes 196
  84.6 21.9 %all-to-all-start.3 = ((f32[12,56,128]{2,1,0:T(8,128)}), f32[12,56,128]{2,1,0:T(8,128)S(1)}, u32[]{:S(2)}, u32[]{:S(2)}) async-start(f32[12,56,128]{2,1,0:T(8,128)} %get-tuple-element.33), calls=%async_computation.3 | async-start | bytes 688128 | tf_op jit(solution)/shard_map/all_to_all | solution.py:309
  88.1 3.1 %collective-permute-start.1 = (f32[8,16,128]{2,1,0:T(8,128)S(1)}, f32[8,16,128]{2,1,0:T(8,128)S(1)}, u32[]{:S(2)}, u32[]{:S(2)}) collective-permute-start(f32[8,16,128]{2,1,0:T(8,128)S(1)} %get-tuple-element.28), channel_id=1, source_target_pairs={{0,1},{1,0},{2,3},{3,2},{4,5},{5,4},{6,7},{7,6},{8,9},{9,8},{10,11... | collective-permute-start | bytes 196616 | tf_op jit(solution)/shard_map/ppermute | solution.py:305
  91.2 9.2 %collective-permute-start.2 = (f32[2,5,16,128]{3,2,1,0:T(8,128)S(1)}, f32[2,5,16,128]{3,2,1,0:T(8,128)S(1)}, u32[]{:S(2)}, u32[]{:S(2)}) collective-permute-start(f32[2,5,16,128]{3,2,1,0:T(8,128)S(1)} %get-tuple-element.30), channel_id=1, source_target_pairs={{0,2},{2,4},{4,6},{6,0},{1,3},{3,5},{5,7},{7,1},{8,10},{10,12},{12... | collective-permute-start | bytes 245768 | tf_op jit(solution)/shard_map/ppermute | solution.py:354
  93.7 7.8 %collective-permute-start.3 = (f32[2,5,16,128]{3,2,1,0:T(8,128)S(1)}, f32[2,5,16,128]{3,2,1,0:T(8,128)S(1)}, u32[]{:S(2)}, u32[]{:S(2)}) collective-permute-start(f32[2,5,16,128]{3,2,1,0:T(8,128)S(1)} %get-tuple-element.31), channel_id=1, source_target_pairs={{0,4},{2,6},{4,0},{6,2},{1,5},{3,7},{5,1},{7,3},{8,12},{10,14},{12... | collective-permute-start | bytes 245768 | tf_op jit(solution)/shard_map/ppermute | solution.py:354
  97.7 6.3 %collective-permute-start.4 = (f32[2,5,16,128]{3,2,1,0:T(8,128)S(1)}, f32[2,5,16,128]{3,2,1,0:T(8,128)S(1)}, u32[]{:S(2)}, u32[]{:S(2)}) collective-permute-start(f32[2,5,16,128]{3,2,1,0:T(8,128)S(1)} %get-tuple-element.32), channel_id=1, source_target_pairs={{0,6},{2,0},{4,2},{6,4},{1,7},{3,1},{5,3},{7,5},{8,14},{10,8},{12,... | collective-permute-start | bytes 245768 | tf_op jit(solution)/shard_map/ppermute | solution.py:354

commit v7 on v5

--- a/solution.py
+++ b/solution.py
@@ -69,6 +69,10 @@
         terms.append(value.astype(jnp.bfloat16))
         value = value - terms[-1].astype(jnp.float32)
     return terms
+
+
+def low_dot(a, b):
+    return lax.dot_general(a, b, TN, preferred_element_type=jnp.float32)
 
 
 def thin_dot(thin, terms, dims):
@@ -277,7 +281,8 @@
     refs = [(ref, c) for ref in (m0_ref, m1_ref, m2_ref, m3_ref) for c in range(NC)]
     mix = jnp.concatenate([ref[c, 0] for ref, c in refs], axis=0)
     left = [jnp.concatenate([ref[c, 1 + r] for ref, c in refs], axis=0) for r in range(4)]
-    grads = hi_dot(mix, jnp.concatenate(left, axis=1), TN)
+    (mix, mix_low), (left, left_low) = split(mix, 2), split(jnp.concatenate(left, axis=1), 2)
+    grads = low_dot(mix_low, left) + low_dot(mix, left_low) + low_dot(mix, left)
     for y in range(NY):
         out_ref[y] = narrow(grads[y * SHARD : (y + 1) * SHARD])
 

time: 122 us -> 122 us (level)
  no operation moved by 1% of the time
where the time goes in v7:
time: 122 us; the launch traced here: 121 us
  blocking collectives  85 us (70%)
  starting transfers between devices  16.6 us (14%)
  Pallas kernels  10.8 us (9%)
  waiting for transfers between devices  7.46 us (6%)
  between operations  1.37 us (1%)
    all_to_all x4, blocking collectives, exchange(): return lax.all_to_all(pieces, axis, 0, 0)  85 us
    ppermute x3, starting transfers between devices, body(): lax.ppermute(messages[k], 'x', [(i, (i + k) % NX) for i in range(NX)])  9.17 us
    pallas_call x1, Pallas kernels, body(): call(pair_kernel, (f32(DOM, BACK, LANES), f32(8, SHARD, LANES), f32(8, SH...  5.64 us
    ppermute x2, starting transfers between devices, swap_core(): return lax.ppermute(piece, 'c', [(0, 1), (1, 0)])  3.95 us
    ppermute x3, waiting for transfers between devices, body(): lax.ppermute(messages[k], 'x', [(i, (i + k) % NX) for i in range(NX)])  3.59 us
    all_to_all x1, starting transfers between devices, exchange(): return lax.all_to_all(pieces, axis, 0, 0)  3.48 us
  transfers between devices with their start and end apart: 6, of which 5 were waited for; matrix products, arithmetic and copies ran while one was open for 0% of the time, Pallas kernels for 2%

profile of v7, /device:TPU:64, one launch (start us, length us, event | category | flops | bytes accessed | tf_op | source)
XLA Modules:
  0.0 121.3 jit_solution(9522347530724514768)
XLA Ops:
  1.3 1.9 %pack.1 = f32[12,16,512]{2,1,0:T(8,128)} custom-call(s32[1,1]{1,0:T(1,128)S(6)} %copy.9.count_hbm, f32[16,400]{1,0:T(8,128)} %emb_ref.1, s32[1,1,512]{2,1,0:T(1,128)} %src_hbm.1, s32[1,1,512]{2,1,0:T(1,128)} %dst_hbm.1, s32[1,1,512]{2,1,0:T(1,128)} %neg_hbm.1, s32[12]{0:T(128)} %plan_hbm.1), custom_call_target="tpu_custom_call" | custom-call | tf_op jit(solution)/shard_map/pack/pallas_call | solution.py:317
  3.1 34.6 %all_to_all.25.came_ref = f32[12,16,512]{2,1,0:T(8,128)S(1)} all-to-all(f32[12,16,512]{2,1,0:T(8,128)} %pack.1), channel_id=1, replica_groups=mesh['dom'=12,'y'=8,'x'=4,'c'=2] {'dom'}, dimensions={0} | all-to-all | bytes 786432 | tf_op jit(solution)/shard_map/all_to_all | solution.py:312
  37.8 0.1 join.1
  37.9 18.9 %all_to_all.26 = f32[8,16,512]{2,1,0:T(8,128)S(1)} all-to-all(f32[8,16,512]{2,1,0:T(8,128)S(1)} %get-tuple-element.19), channel_id=1, replica_groups=mesh['dom'=12,'y'=8,'x'=4,'c'=2] {'y'}, dimensions={0} | all-to-all | bytes 524288 | tf_op jit(solution)/shard_map/all_to_all | solution.py:312
  56.8 0.1 broadcast_in_dim.11
  56.9 17.6 %all_to_all.27 = f32[4,128,512]{2,1,0:T(8,128)S(1)} all-to-all(f32[4,128,512]{2,1,0:T(8,128)S(1)} %broadcast_in_dim.11), channel_id=1, replica_groups=mesh['dom'=12,'y'=8,'x'=4,'c'=2] {'x'}, dimensions={0} | all-to-all | bytes 2097152 | tf_op jit(solution)/shard_map/all_to_all | solution.py:312
  74.5 1.9 %collective-permute-start = (f32[4,128,512]{2,1,0:T(8,128)S(1)}, f32[4,128,512]{2,1,0:T(8,128)S(1)}, u32[]{:S(2)}, u32[]{:S(2)}) collective-permute-start(f32[4,128,512]{2,1,0:T(8,128)S(1)} %all_to_all.27), channel_id=1, source_target_pairs={{0,1},{1,0},{2,3},{3,2},{4,5},{5,4},{6,7},{7,6},{8,9},{9,8},{10,11... | collective-permute-start | bytes 3145736 | tf_op jit(solution)/shard_map/ppermute | solution.py:308
  76.5 1.9 %edges.1 = (f32[32,8,16,128]{3,2,1,0:T(8,128)S(1)}, f32[32,8,128]{2,1,0:T(8,128)S(1)}, f32[16,512]{1,0:T(8,128)S(1)}) custom-call(f32[16,512]{1,0:T(8,128)S(1)} %get-tuple-element.18.left_ref, f32[32,16,512]{2,1,0:T(8,128)S(1)} %bitcast.6), custom_call_target="tpu_custom_call" | custom-call | tf_op jit(solution)/shard_map/edges/pallas_call | solution.py:336
  78.4 0.7 collective-permute-done
  79.1 5.6 %pair.1 = (f32[12,56,128]{2,1,0:T(8,128)}, f32[8,16,128]{2,1,0:T(8,128)S(1)}, f32[8,16,128]{2,1,0:T(8,128)S(1)}) custom-call(f32[16,512]{1,0:T(8,128)S(1)} %get-tuple-element.18.left_ref, f32[32,16,512]{2,1,0:T(8,128)S(1)} %bitcast.7, f32[32,16,512]{2,1,0:T(8,128)S(1)} %bitcast.8, f32[32,8,16,128]{3,2,1,0:T(8,128)S(1)} %get-tuple-element.20.e0_ref, ...), custom_call_target="tpu_custom_call" | custom-call | tf_op jit(solution)/shard_map/pair/pallas_call | solution.py:343
  84.7 3.5 %all-to-all-start.3 = ((f32[12,56,128]{2,1,0:T(8,128)}), f32[12,56,128]{2,1,0:T(8,128)S(1)}, u32[]{:S(2)}, u32[]{:S(2)}) async-start(f32[12,56,128]{2,1,0:T(8,128)} %get-tuple-element.29), calls=%async_computation.3 | async-start | bytes 688128 | tf_op jit(solution)/shard_map/all_to_all | solution.py:312
  88.2 2.0 %collective-permute-start.1 = (f32[8,16,128]{2,1,0:T(8,128)S(1)}, f32[8,16,128]{2,1,0:T(8,128)S(1)}, u32[]{:S(2)}, u32[]{:S(2)}) collective-permute-start(f32[8,16,128]{2,1,0:T(8,128)S(1)} %get-tuple-element.24), channel_id=1, source_target_pairs={{0,1},{1,0},{2,3},{3,2},{4,5},{5,4},{6,7},{7,6},{8,9},{9,8},{10,11... | collective-permute-start | bytes 196616 | tf_op jit(solution)/shard_map/ppermute | solution.py:308
  90.3 1.1 collective-permute-done.1.came_ref
  91.4 2.5 %collective-permute-start.2 = (f32[2,5,16,128]{3,2,1,0:T(8,128)S(1)}, f32[2,5,16,128]{3,2,1,0:T(8,128)S(1)}, u32[]{:S(2)}, u32[]{:S(2)}) collective-permute-start(f32[2,5,16,128]{3,2,1,0:T(8,128)S(1)} %get-tuple-element.26), channel_id=1, source_target_pairs={{0,2},{2,4},{4,6},{6,0},{1,3},{3,5},{5,7},{7,1},{8,10},{10,12},{12... | collective-permute-start | bytes 245768 | tf_op jit(solution)/shard_map/ppermute | solution.py:356
  93.9 4.0 %collective-permute-start.3 = (f32[2,5,16,128]{3,2,1,0:T(8,128)S(1)}, f32[2,5,16,128]{3,2,1,0:T(8,128)S(1)}, u32[]{:S(2)}, u32[]{:S(2)}) collective-permute-start(f32[2,5,16,128]{3,2,1,0:T(8,128)S(1)} %get-tuple-element.27), channel_id=1, source_target_pairs={{0,4},{2,6},{4,0},{6,2},{1,5},{3,7},{5,1},{7,3},{8,12},{10,14},{12... | collective-permute-start | bytes 245768 | tf_op jit(solution)/shard_map/ppermute | solution.py:356
  97.8 2.7 %collective-permute-start.4 = (f32[2,5,16,128]{3,2,1,0:T(8,128)S(1)}, f32[2,5,16,128]{3,2,1,0:T(8,128)S(1)}, u32[]{:S(2)}, u32[]{:S(2)}) collective-permute-start(f32[2,5,16,128]{3,2,1,0:T(8,128)S(1)} %get-tuple-element.28), channel_id=1, source_target_pairs={{0,6},{2,0},{4,2},{6,4},{1,7},{3,1},{5,3},{7,5},{8,14},{10,8},{12,... | collective-permute-start | bytes 245768 | tf_op jit(solution)/shard_map/ppermute | solution.py:356
  100.6 0.0 collective-permute-done.2.m1_ref
  100.6 1.1 collective-permute-done.3.m2_ref
  101.7 2.5 %collective-permute-done.4.m3_ref = f32[2,5,16,128]{3,2,1,0:T(8,128)S(1)} collective-permute-done((f32[2,5,16,128]{3,2,1,0:T(8,128)S(1)}, f32[2,5,16,128]{3,2,1,0:T(8,128)S(1)}, u32[]{:S(2)}, u32[]{:S(2)}) %collective-permute-start.4) | collective-permute-done | bytes 81952 | tf_op jit(solution)/shard_map/ppermute | solution.py:356
  104.2 0.3 right.1
  104.5 2.1 %all-to-all-done.3.back_ref = f32[12,56,128]{2,1,0:T(8,128)S(1)} async-done(((f32[12,56,128]{2,1,0:T(8,128)}), f32[12,56,128]{2,1,0:T(8,128)S(1)}, u32[]{:S(2)}, u32[]{:S(2)}) %all-to-all-start.3) | async-done | bytes 344096 | tf_op jit(solution)/shard_map/all_to_all | solution.py:312
  106.6 13.8 %all_to_all.28.right_ref = f32[8,56,128]{2,1,0:T(8,128)S(1)} all-to-all(f32[8,56,128]{2,1,0:T(8,128)S(1)} %right.1), channel_id=1, replica_groups=mesh['dom'=12,'y'=8,'x'=4,'c'=2] {'y'}, dimensions={0} | all-to-all | bytes 458752 | tf_op jit(solution)/shard_map/all_to_all | solution.py:312
  120.4 0.0 copy-done
  120.5 0.9 finish.1
  (6 shorter events, 0.0 us)
Async XLA Ops:
  74.5 4.5 %collective-permute-start = (f32[4,128,512]{2,1,0:T(8,128)S(1)}, f32[4,128,512]{2,1,0:T(8,128)S(1)}, u32[]{:S(2)}, u32[]{:S(2)}) collective-permute-start(f32[4,128,512]{2,1,0:T(8,128)S(1)} %all_to_all.27), channel_id=1, source_target_pairs={{0,1},{1,0},{2,3},{3,2},{4,5},{5,4},{6,7},{7,6},{8,9},{9,8},{10,11... | collective-permute-start | bytes 3145736 | tf_op jit(solution)/shard_map/ppermute | solution.py:308
  79.1 41.4 %copy-start = (f32[16,400]{1,0:T(8,128)S(1)}, f32[16,400]{1,0:T(8,128)}, u32[]{:S(2)}) copy-start(f32[16,400]{1,0:T(8,128)} %emb_ref.1) | copy-start | bytes 76804
  79.1 41.4 %copy-start.1 = (s32[12]{0:T(128)S(1)}, s32[12]{0:T(128)}, u32[]{:S(2)}) copy-start(s32[12]{0:T(128)} %plan_hbm.1) | copy-start | bytes 148
  79.1 41.4 %copy-start.2 = (f32[16]{0:T(128)S(1)}, f32[16]{0:T(128)}, u32[]{:S(2)}) copy-start(f32[16]{0:T(128)} %param.8) | copy-start | bytes 196
  84.7 21.9 %all-to-all-start.3 = ((f32[12,56,128]{2,1,0:T(8,128)}), f32[12,56,128]{2,1,0:T(8,128)S(1)}, u32[]{:S(2)}, u32[]{:S(2)}) async-start(f32[12,56,128]{2,1,0:T(8,128)} %get-tuple-element.29), calls=%async_computation.3 | async-start | bytes 688128 | tf_op jit(solution)/shard_map/all_to_all | solution.py:312
  88.2 3.1 %collective-permute-start.1 = (f32[8,16,128]{2,1,0:T(8,128)S(1)}, f32[8,16,128]{2,1,0:T(8,128)S(1)}, u32[]{:S(2)}, u32[]{:S(2)}) collective-permute-start(f32[8,16,128]{2,1,0:T(8,128)S(1)} %get-tuple-element.24), channel_id=1, source_target_pairs={{0,1},{1,0},{2,3},{3,2},{4,5},{5,4},{6,7},{7,6},{8,9},{9,8},{10,11... | collective-permute-start | bytes 196616 | tf_op jit(solution)/shard_map/ppermute | solution.py:308
  91.4 9.2 %collective-permute-start.2 = (f32[2,5,16,128]{3,2,1,0:T(8,128)S(1)}, f32[2,5,16,128]{3,2,1,0:T(8,128)S(1)}, u32[]{:S(2)}, u32[]{:S(2)}) collective-permute-start(f32[2,5,16,128]{3,2,1,0:T(8,128)S(1)} %get-tuple-element.26), channel_id=1, source_target_pairs={{0,2},{2,4},{4,6},{6,0},{1,3},{3,5},{5,7},{7,1},{8,10},{10,12},{12... | collective-permute-start | bytes 245768 | tf_op jit(solution)/shard_map/ppermute | solution.py:356
  93.9 7.8 %collective-permute-start.3 = (f32[2,5,16,128]{3,2,1,0:T(8,128)S(1)}, f32[2,5,16,128]{3,2,1,0:T(8,128)S(1)}, u32[]{:S(2)}, u32[]{:S(2)}) collective-permute-start(f32[2,5,16,128]{3,2,1,0:T(8,128)S(1)} %get-tuple-element.27), channel_id=1, source_target_pairs={{0,4},{2,6},{4,0},{6,2},{1,5},{3,7},{5,1},{7,3},{8,12},{10,14},{12... | collective-permute-start | bytes 245768 | tf_op jit(solution)/shard_map/ppermute | solution.py:356
  97.8 6.3 %collective-permute-start.4 = (f32[2,5,16,128]{3,2,1,0:T(8,128)S(1)}, f32[2,5,16,128]{3,2,1,0:T(8,128)S(1)}, u32[]{:S(2)}, u32[]{:S(2)}) collective-permute-start(f32[2,5,16,128]{3,2,1,0:T(8,128)S(1)} %get-tuple-element.28), channel_id=1, source_target_pairs={{0,6},{2,0},{4,2},{6,4},{1,7},{3,1},{5,3},{7,5},{8,14},{10,8},{12,... | collective-permute-start | bytes 245768 | tf_op jit(solution)/shard_map/ppermute | solution.py:356
